TPU v7x, 256 devices: a whole 4x4x8 slice. The times are simulated.
256 devices in a mesh: roll: 32 (over y, x, core), mp: 8 (over z).
Axes of the slice: x: 4, y: 4, z: 8, core: 2. Of those that a mesh axis runs over, the one named last changes fastest.
Arguments:
- tokens: bfloat16 [12288, 5120], P('roll', 'mp'), may hold values from -24 to 24
- dest_shard: int32 [12288], P('roll'), may hold values from 0 to 31, as said below
- dest_offset: int32 [12288], P('roll'), may hold values from 0 to 383, as said below
- seg_lengths: int32 [32, 4], P('roll'), may hold values from 1 to 192, 384 in all within a row
- rewards: int32 [128], P('roll'), may hold values from 0 to 19
- groups: int32 [128], P('roll'), may hold values from 0 to 7, as said below
- reference_head_weight: bfloat16 [5120, 8, 640], P('roll', 'mp'), may hold values from -0.078125 to 0.078125
- policy_head_weight: bfloat16 [5120, 8, 640], P('roll', 'mp'), may hold values from -0.078125 to 0.078125
- upstream: bfloat16 [12288, 8, 384], P('roll', 'mp'), may hold values from -6 to 6
Outputs:
- grad_policy: float32 [5120, 8, 640], P('roll', 'mp')
Inputs may be any that keep to these rules, and one draw needn't show every extreme that they name: `dest_shard`: one rollout worker sends at most 24 rows to one trainer shard, and exactly 24 to some; every trainer shard receives exactly 384 rows. `dest_offset`: the rows bound for one trainer shard have distinct offsets. `groups`: every prompt has exactly 16 responses.
All inputs are finite; a program needn't handle non-finite values.
Results may differ from a plain program's by a relative error of at most 0.02.
The roundings to bfloat16 on the way count: a program that leaves them out, or rounds other values in their place, can miss the bound.
Values may be sent and summed in bfloat16 or wider, within the bound.
No kernel may reach another device: no remote copies, remote signals or barrier semaphores. Data moves between devices by JAX's collectives and lax.ppermute only.
A program may use at most 128 MiB of HBM per device.

v0:
```python
import jax
import jax.numpy as jnp
from jax import lax
from jax.experimental import pallas as pl
from jax.experimental.pallas import tpu as pltpu
from jax.sharding import Mesh
from jax.sharding import PartitionSpec as P

HEAD_WIDTH = 128
KL_WEIGHT = 1.0
MASKED_SCORE = -1e30

ROWS = 384
CAP = 24
MODEL_BLOCK = 640
COLS = 640
CHUNK = 160
HALF = 2 * CHUNK
LANES = 384
F32 = jnp.float32
BF16 = jnp.bfloat16
I32 = jnp.int32

REWARDS, GROUPS, LENGTHS = 4, 8, 12
NOTE_HIGH, NOTE_LOW, NOTE_REWARD, NOTE_GROUP = 64, 65, 66, 70

VMEM = pl.BlockSpec(memory_space=pltpu.VMEM)
SMEM = pl.BlockSpec(memory_space=pltpu.SMEM)
HBM = pl.BlockSpec(memory_space=pltpu.HBM)
ALONE = pltpu.CompilerParams(vmem_limit_bytes=60 * 1024 * 1024)
PARAMS = pltpu.CompilerParams(vmem_limit_bytes=28 * 1024 * 1024)


def iota(shape, dim):
    return lax.broadcasted_iota(I32, shape, dim)


def dot(a, b, contract=((1,), (0,))):
    return lax.dot_general(a, b, (contract, ((), ())), preferred_element_type=F32)


def fetch(pairs, semaphores):
    copies = [pltpu.make_async_copy(source, to, semaphores.at[i]) for i, (source, to) in enumerate(pairs)]
    for copy in copies:
        copy.start()
    return copies


def shift(value, axis, size, by):
    return lax.ppermute(value, axis, [(i, (i + by) % size) for i in range(size)])


def turned(value, first, by):
    pairs = []
    for y in range(4):
        for x in range(4):
            for c in range(2):
                to_y, to_x = (y, (x + by) % 4) if (c == 0) == first else ((y + by) % 4, x)
                pairs.append((8 * y + 2 * x + c, 8 * to_y + 2 * to_x + c))
    return lax.ppermute(value, ("y", "x", "c"), pairs)


def turned_place(where):
    y, x, odd = where[0], where[1], where[2]
    first = jnp.where(odd == 0, x, y)
    second = jnp.where(odd == 0, y, x)
    stride = jnp.where(odd == 0, 1, 4)
    return first, second, stride, 5 - stride


def wrapped(index, size):
    return lax.rem(index + size, size)


def route_kernel(rewards, groups, shard, offset, tokens, out, landed, semaphores):
    copy = fetch([(tokens, landed)], semaphores)[0]
    shard_row = shard[...].reshape(1, ROWS)
    offset_row = offset[...].reshape(1, ROWS)
    table = iota((32, ROWS), 0) == shard_row
    before = (iota((ROWS, ROWS), 0) < iota((ROWS, ROWS), 1)).astype(BF16)
    counts = dot(table.astype(BF16), before)
    rank = jnp.sum(jnp.where(table, counts, 0.0), axis=0, keepdims=True).astype(I32)
    slot = shard_row * CAP + rank
    hot = iota((32 * CAP, ROWS), 0) == slot
    lane = iota((MODEL_BLOCK, 2 * LANES), 1)
    half = (lane >= LANES).astype(I32)
    within = lane - half * LANES
    source = jnp.where(within < CHUNK, within, within + CHUNK) + CHUNK * half
    pick = (iota((MODEL_BLOCK, 2 * LANES), 0) == source) & (within < HALF)
    copy.wait()
    ordered = dot(landed[...], pick.astype(BF16)).astype(BF16)
    gathered = dot(hot.astype(BF16), ordered)
    odd = shard_row & 1
    note_lane = iota((1, 128), 1)
    common = jnp.zeros((1, 128), F32)
    for i in range(4):
        common = jnp.where(note_lane == NOTE_REWARD + i, rewards[i].astype(F32), common)
        common = jnp.where(note_lane == NOTE_GROUP + i, groups[i].astype(F32), common)
    for core in range(2):
        place = offset_row + 1 + ROWS * (odd ^ core)
        mark = jnp.sum(jnp.where(hot, place, 0), axis=1, keepdims=True)
        high = (mark >> 4).astype(F32)
        low = (mark & 15).astype(F32)
        notes = jnp.where(note_lane == NOTE_HIGH, high, jnp.where(note_lane == NOTE_LOW, low, common))
        first = LANES * core
        plain = gathered[:, first : first + 256].astype(BF16)
        last = (gathered[:, first + 256 : first + 384] + notes).astype(BF16)
        for chip in range(16):
            rows = slice(2 * CAP * chip, 2 * CAP * (chip + 1))
            out[2 * chip + core, :, 0:256] = plain[rows]
            out[2 * chip + core, :, 256:384] = last[rows]


def route(rewards, groups, shard, offset, tokens):
    return pl.pallas_call(
        route_kernel,
        out_shape=jax.ShapeDtypeStruct((32, 2 * CAP, LANES), BF16),
        in_specs=[SMEM, SMEM, VMEM, VMEM, HBM],
        out_specs=VMEM,
        scratch_shapes=[pltpu.VMEM((ROWS, MODEL_BLOCK), BF16), pltpu.SemaphoreType.DMA((1,))],
        compiler_params=ALONE,
        name="route",
    )(rewards, groups, shard, offset, tokens)


def place_kernel(arrived, out):
    rows = arrived[...].reshape(32 * 2 * CAP, LANES)
    notes = rows[:, 256:384].astype(F32)
    note_lane = iota((1, 128), 1)
    weight = jnp.where(note_lane == NOTE_HIGH, 16.0, jnp.where(note_lane == NOTE_LOW, 1.0, 0.0))
    mark = jnp.sum(notes * weight, axis=1, keepdims=True).astype(I32) - 1
    hot = (mark == iota((32 * 2 * CAP, 2 * ROWS), 1)).astype(BF16)
    out[...] = dot(rows, hot, ((0,), (0,)))[:HALF].astype(BF16)


def place(arrived):
    return pl.pallas_call(
        place_kernel,
        out_shape=jax.ShapeDtypeStruct((HALF, 2 * ROWS), BF16),
        in_specs=[VMEM],
        out_specs=VMEM,
        compiler_params=PARAMS,
        name="place",
    )(arrived)


def row_advantages(reward, group, small):
    position = iota((ROWS, 128), 0)
    result = jnp.zeros((ROWS, 128), F32)
    start = 0
    for i in range(4):
        member = group == small[GROUPS + i].astype(F32)
        count = jnp.sum(jnp.where(member, 1.0, 0.0), keepdims=True)
        total = jnp.sum(jnp.where(member, reward, 0.0), keepdims=True)
        square = jnp.sum(jnp.where(member, reward * reward, 0.0), keepdims=True)
        mean = total / count
        spread = jnp.maximum(jnp.sqrt(count * square - total * total) / count, 1.0)
        advantage = (small[REWARDS + i].astype(F32) - mean) / spread
        result = jnp.where(position >= start, advantage, result)
        start = start + small[LENGTHS + i]
    return result


def stack(pieces, out):
    at = 0
    for piece in pieces:
        out[at : at + piece.shape[0], :] = piece[...]
        at += piece.shape[0]


def join_kernel(*refs):
    stack(refs[:-1], refs[-1])


def join(pieces):
    return pl.pallas_call(
        join_kernel,
        out_shape=jax.ShapeDtypeStruct((4 * CHUNK, 2 * COLS), BF16),
        in_specs=[VMEM] * 4,
        out_specs=VMEM,
        compiler_params=PARAMS,
        name="join",
    )(*pieces)


STEPS = (-2, -1, 0, 1, 2, 3, -3, 4)


def slot_of(chunk, z):
    at = wrapped(lax.div(chunk, 2) - z + 2, 8)
    at = jnp.where(at == 6, 7, jnp.where(at == 7, 6, at))
    return pl.multiple_of((2 * at + lax.rem(chunk, 2)) * CHUNK, 16)


def chunk_rows(parts, slot):
    total = None
    for part, begin in parts:
        inside = (slot >= begin) & (slot < begin + part.shape[0])
        at = pl.multiple_of(jnp.where(inside, slot - begin, 0), 16)
        rows = part[pl.ds(at, CHUNK), :]
        rows = jnp.where(inside, rows, jnp.zeros_like(rows))
        total = rows if total is None else total + rows
    return total


def chunk_slots(where, step):
    first, second, first_stride, second_stride = turned_place(where)
    at = wrapped(second + step, 4) * second_stride
    return [slot_of(wrapped(first + near, 4) * first_stride + at, where[3]) for near in (0, -1, 1, 2)]


def chunk_slot(where, step, k):
    first, second, first_stride, second_stride = turned_place(where)
    near = jnp.where(k == 0, 0, jnp.where(k == 1, -1, k - 1))
    chunk = wrapped(first + near, 4) * first_stride + wrapped(second + step, 4) * second_stride
    return slot_of(chunk, where[3])


def keep_late(where, step, piece, late):
    def keep(k, carry):
        slot = chunk_slot(where, step, k)

        @pl.when(slot >= 7 * HALF)
        def _():
            at = pl.ds(pl.multiple_of(slot - 7 * HALF, 16), CHUNK)
            late[at, :] = piece[pl.ds(pl.multiple_of(k * CHUNK, 16), CHUNK), :]

        return carry

    lax.fori_loop(0, 4, keep, 0)


def project_kernel(where, arrived, *refs):
    tokens, piece = refs[:5], refs[5]
    own, other, late, advantage, whole = refs[6:]
    note = arrived[:, 0:16, 256:384][:, 0, :].astype(F32)
    advantage[...] = row_advantages(
        note[:, NOTE_REWARD : NOTE_REWARD + 4], note[:, NOTE_GROUP : NOTE_GROUP + 4], where
    )
    stack(tokens, whole)
    keep_late(where, 0, piece, late)
    rows = [chunk_rows([(whole, 0)], slot) for slot in chunk_slots(where, 0)]
    rows = jnp.concatenate(rows, axis=0)
    own[...] = dot(rows[:, :ROWS], piece[...], ((0,), (0,)))
    other[...] = dot(rows[:, ROWS:], piece[...], ((0,), (0,)))


SUMS = jax.ShapeDtypeStruct((ROWS, 2 * COLS), F32)
LATE = jax.ShapeDtypeStruct((HALF, 2 * COLS), BF16)


def project(where, arrived, tokens, piece):
    whole = jax.ShapeDtypeStruct((5 * HALF, 2 * ROWS), BF16)
    return pl.pallas_call(
        project_kernel,
        out_shape=(SUMS, SUMS, LATE, jax.ShapeDtypeStruct((ROWS, 128), F32), whole),
        in_specs=[SMEM] + [VMEM] * 7,
        out_specs=(VMEM,) * 5,
        compiler_params=PARAMS,
        name="project",
    )(where, arrived, *tokens, piece)


def far_kernel(where, own, other, *refs):
    tokens, piece = refs[:2], refs[2]
    own_out, other_out, far = refs[3:]
    stack(tokens, far)
    own_out[...] = own[...]
    other_out[...] = other[...]

    def add(k, carry):
        slot = chunk_slot(where, 0, k)

        @pl.when((slot >= 5 * HALF) & (slot < 7 * HALF))
        def _():
            at = pl.ds(pl.multiple_of(slot - 5 * HALF, 16), CHUNK)
            weights = piece[pl.ds(pl.multiple_of(k * CHUNK, 16), CHUNK), :]
            own_out[...] += dot(far[at, :ROWS], weights, ((0,), (0,)))
            other_out[...] += dot(far[at, ROWS:], weights, ((0,), (0,)))

        return carry

    lax.fori_loop(0, 4, add, 0)


def project_far(where, own, other, tokens, piece):
    far = jax.ShapeDtypeStruct((2 * HALF, 2 * ROWS), BF16)
    return pl.pallas_call(
        far_kernel,
        out_shape=(SUMS, SUMS, far),
        in_specs=[SMEM] + [VMEM] * 5,
        out_specs=(VMEM,) * 3,
        compiler_params=PARAMS,
        name="far",
    )(where, own, other, *tokens, piece)


def across_sum(where, columns, whole, far, pieces):
    total = None
    for piece, step in zip(pieces, (-1, 1, 2)):
        parts = [(whole.at[:, columns], 0), (far.at[:, columns], 5 * HALF)]
        rows = jnp.concatenate([chunk_rows(parts, slot) for slot in chunk_slots(where, step)], axis=0)
        result = dot(rows, piece[...], ((0,), (0,)))
        total = result if total is None else total + result
    return total


def across_other(where, other, late, whole, far, pieces):
    def kernel(where, other, late, whole, far, *refs):
        pieces, (out, late_out) = refs[:3], refs[3:]
        late_out[...] = late[...]
        for piece, step in zip(pieces, (-1, 1, 2)):
            keep_late(where, step, piece, late_out)
        out[...] = other[...] + across_sum(where, pl.ds(ROWS, ROWS), whole, far, pieces)

    return pl.pallas_call(
        kernel,
        out_shape=(SUMS, LATE),
        in_specs=[SMEM] + [VMEM] * 7,
        out_specs=(VMEM,) * 2,
        compiler_params=PARAMS,
        name="across_other",
    )(where, other, late, whole, far, *pieces)


def late_other(other, late, first, second):
    def kernel(other, late, first, second, out, tokens):
        stack([first, second], tokens)
        out[...] = other[...] + dot(tokens[:, ROWS:], late[...], ((0,), (0,)))

    return pl.pallas_call(
        kernel,
        out_shape=(SUMS, jax.ShapeDtypeStruct((HALF, 2 * ROWS), BF16)),
        in_specs=[VMEM] * 4,
        out_specs=(VMEM,) * 2,
        compiler_params=PARAMS,
        name="late",
    )(other, late, first, second)


def across_own(where, own, late, whole, far, last, pieces):
    def kernel(where, own, late, whole, far, last, *refs):
        pieces, out = refs[:3], refs[3]
        total = across_sum(where, pl.ds(0, ROWS), whole, far, pieces)
        out[...] = own[...] + total + dot(last[:, :ROWS], late[...], ((0,), (0,)))

    return pl.pallas_call(
        kernel,
        out_shape=SUMS,
        in_specs=[SMEM] + [VMEM] * 8,
        out_specs=VMEM,
        compiler_params=PARAMS,
        name="across_own",
    )(where, own, late, whole, far, last, *pieces)


def heads(value):
    return jnp.concatenate([value[:, 128 * i : 128 * (i + 1)] for i in range(3)], axis=0)


def attend(small, projection, block):
    first, count = 128 * block, 128 * (block + 1)
    key_at = iota((128, count), 1)
    query_at = first + iota((128, count), 0)
    row_at = first + iota((128, 1), 0)
    begin = jnp.zeros((128, 1), I32)
    start = 0
    for i in range(4):
        begin = jnp.where(row_at >= start, start, begin)
        start = start + small[LENGTHS + i]
    allowed = (key_at <= query_at) & (key_at >= begin)
    allowed = jnp.concatenate([allowed] * 3, axis=0)
    queries = heads(projection[first:count, 0:384])
    keys, values = projection[:count, 384:512], projection[:count, 512:640]
    scores = dot(queries, keys, ((1,), (1,))) * HEAD_WIDTH**-0.5
    scores = jnp.where(allowed, scores, MASKED_SCORE)
    weights = jnp.exp(scores - jnp.max(scores, axis=1, keepdims=True))
    probs = weights / jnp.sum(weights, axis=1, keepdims=True)
    rounded = probs.astype(BF16)
    return queries, keys, values, probs, rounded, dot(rounded, values)


def two_parts(value):
    high = value.astype(BF16)
    return high, (value - high.astype(F32)).astype(BF16)


def attention_kernel(small, own, received, upstream, advantage, out):
    scale = HEAD_WIDTH**-0.5
    projection = (own[...] + received[...]).astype(BF16)
    ref_projection, projection = projection[:, :COLS], projection[:, COLS:]
    grad_keys, grad_values = [0.0] * 3, [0.0] * 3
    for block in range(3):
        rows = slice(128 * block, 128 * (block + 1))
        out_ref = attend(small, ref_projection, block)[5]
        queries, keys, values, probs, rounded, out_policy = attend(small, projection, block)
        weight = jnp.concatenate([advantage[rows, :]] * 3, axis=0)
        grad_out = weight * heads(upstream[rows, :].astype(F32))
        grad_out = grad_out + KL_WEIGHT * (out_policy - out_ref)
        high, low = two_parts(grad_out * 12288**-0.5)
        grad_probs = dot(high, values, ((1,), (1,))) + dot(low, values, ((1,), (1,)))
        grad_scores = probs * (grad_probs - jnp.sum(grad_probs * probs, axis=1, keepdims=True))
        grad_scores = (grad_scores * scale).astype(BF16)
        grad_query = dot(grad_scores, keys)
        for i in range(3):
            out[rows, 128 * i : 128 * (i + 1)] = grad_query[128 * i : 128 * (i + 1)].astype(BF16)
        for_keys = dot(grad_scores, queries, ((0,), (0,)))
        for_values = dot(rounded, high, ((0,), (0,)))
        for k in range(block + 1):
            grad_keys[k] = grad_keys[k] + for_keys[128 * k : 128 * (k + 1)]
            grad_values[k] = grad_values[k] + for_values[128 * k : 128 * (k + 1)]
    for k in range(3):
        out[128 * k : 128 * (k + 1), 384:512] = grad_keys[k].astype(BF16)
        out[128 * k : 128 * (k + 1), 512:640] = grad_values[k].astype(BF16)


def attention(small, own, received, upstream, advantage):
    return pl.pallas_call(
        attention_kernel,
        out_shape=jax.ShapeDtypeStruct((ROWS, COLS), BF16),
        in_specs=[SMEM] + [VMEM] * 4,
        out_specs=VMEM,
        compiler_params=PARAMS,
        name="attention",
    )(small, own, received, upstream, advantage)


def gradient_dot(move, where, whole, far, last, grad):
    first, _, first_stride, second_stride = turned_place(where)
    parts = [(whole, 0), (far, 5 * HALF), (last, 7 * HALF)]
    rows = []
    for k in range(4):
        chunk = wrapped(first + move, 4) * first_stride + k * second_stride
        rows.append(chunk_rows(parts, slot_of(chunk, where[3])))
    return dot(jnp.concatenate(rows, axis=0), grad).astype(BF16)


PART = jax.ShapeDtypeStruct((4 * CHUNK, COLS), BF16)


def gradient_part(where, whole, far, last, own, other, move):
    def kernel(where, whole, far, last, own, other, out):
        grad = jnp.concatenate([own[...], other[...]], axis=0)
        out[...] = gradient_dot(move, where, whole, far, last, grad)

    return pl.pallas_call(
        kernel,
        out_shape=PART,
        in_specs=[SMEM] + [VMEM] * 5,
        out_specs=VMEM,
        compiler_params=PARAMS,
        name="gradient",
    )(where, whole, far, last, own, other)


def middle_kernel(where, own, *refs):
    pieces, outs = refs[:3], refs[3:]
    second = turned_place(where)[1]
    for move, out in zip((0, 1, -1, 2), outs):
        at = pl.ds(pl.multiple_of(wrapped(second + move, 4) * CHUNK, 16), CHUNK)
        total = (own[at, :].astype(F32) + pieces[0][at, :].astype(F32)) + (
            pieces[1][at, :].astype(F32) + pieces[2][at, :].astype(F32)
        )
        out[...] = total.astype(out.dtype)


def middle_sums(where, own, pieces):
    def shape(kind):
        return jax.ShapeDtypeStruct((CHUNK, COLS), kind)

    return pl.pallas_call(
        middle_kernel,
        out_shape=(shape(F32), shape(BF16), shape(BF16), shape(BF16)),
        in_specs=[SMEM] + [VMEM] * 4,
        out_specs=(VMEM,) * 4,
        compiler_params=PARAMS,
        name="middle",
    )(where, own, *pieces)


def final_kernel(own, first, second, third, out):
    out[:, 0, :] = (own[...] + first[...].astype(F32)) + (second[...].astype(F32) + third[...].astype(F32))


def final_sums(own, pieces):
    return pl.pallas_call(
        final_kernel,
        out_shape=jax.ShapeDtypeStruct((CHUNK, 1, COLS), F32),
        in_specs=[VMEM] * 4,
        out_specs=VMEM,
        compiler_params=PARAMS,
        name="final",
    )(own, *pieces)


def body(
    tokens,
    dest_shard,
    dest_offset,
    seg_lengths,
    rewards,
    groups,
    reference_head_weight,
    policy_head_weight,
    upstream,
):
    where = jnp.stack([lax.axis_index(name).astype(I32) for name in ("y", "x", "c", "z")])
    small = jnp.concatenate([where, rewards, groups, seg_lengths[0]])
    outgoing = route(rewards, groups, dest_shard, dest_offset, tokens)
    arrived = lax.all_to_all(outgoing, ("y", "x", "c"), split_axis=0, concat_axis=0, tiled=True)
    arrived, small = lax.optimization_barrier((arrived, small))
    _, weights, policy_weights = lax.optimization_barrier(
        (outgoing, reference_head_weight[:, 0], policy_head_weight[:, 0])
    )
    weights = jnp.concatenate([weights, policy_weights], axis=1)
    near = [weights, *(turned(weights, True, by) for by in (1, -1, 2))]
    block = place(arrived)
    _, near = lax.optimization_barrier((block, near))
    rows = join(near)
    across, right, left = (turned(rows, False, by) for by in (2, 1, -1))
    weights = [right, left, across]

    forward, backward = [block], [block]
    for _ in range(3):
        forward.append(shift(forward[-1], "z", 8, 1))
        backward.append(shift(backward[-1], "z", 8, -1))

    near = [forward[2], forward[1], block, backward[1], backward[2]]
    own, other, late, advantage, whole = project(small, arrived, near, rows)
    far = [backward[3], forward[3]]
    behind, ahead, own = lax.optimization_barrier((*far, own))
    first = shift(ahead[:CHUNK], "z", 8, 1)
    second = shift(behind[CHUNK:], "z", 8, -1)
    own, other, far = project_far(small, own, other, far, rows)
    swap = [(0, 1), (1, 0)]
    other, late = across_other(small, other, late, whole, far, weights)
    other, last = late_other(other, late, first, second)
    received = lax.ppermute(other, "c", swap)
    own = across_own(small, own, late, whole, far, last, weights)
    cotangent = upstream.reshape(ROWS, 3 * HEAD_WIDTH)
    grad = attention(small, own, received, cotangent, advantage)
    grad_other = lax.ppermute(grad, "c", swap)

    parts = []
    for move in (-1, 1, 2, 0):
        part = gradient_part(small, whole, far, last, grad, grad_other, move)
        parts.append(turned(part, True, move) if move else part)
    sums = middle_sums(small, parts[3], parts[:3])
    parts = [turned(part, False, move) for move, part in zip((1, -1, 2), sums[1:])]
    return final_sums(sums[0], parts)


def solution(mesh):
    split = Mesh(mesh.devices.reshape(4, 4, 2, 8), ("y", "x", "c", "z"))
    roll = ("y", "x", "c")
    in_specs = (
        P(roll, "z"),
        P(roll),
        P(roll),
        P(roll, None),
        P(roll),
        P(roll),
        P(roll, "z", None),
        P(roll, "z", None),
        P(roll, "z", None),
    )
    out_specs = P(roll, "z", None)
    return jax.shard_map(body, mesh=split, in_specs=in_specs, out_specs=out_specs, check_vma=False)
```

profile of v0, /device:TPU:8, one launch (start us, length us, event | category | flops | bytes accessed | tf_op | source)
XLA Modules:
  0.0 135.4 jit_solution(15315277695835277992)
XLA Ops:
  0.0 4.2 %route.1 = bf16[32,48,384]{2,1,0:T(8,128)(2,1)} custom-call(s32[4]{0:T(128)} %rewards.1, s32[4]{0:T(128)} %groups.1, s32[384]{0:T(512)} %shard.1, s32[384]{0:T(512)} %offset.1, bf16[384,640]{1,0:T(8,128)(2,1)} %tokens.1), custom_call_target="tpu_custom_call" | custom-call | tf_op jit(solution)/shard_map/route/pallas_call | solution.py:115
  4.2 7.7 %all-to-all-start = ((bf16[32,48,384]{2,1,0:T(8,128)(2,1)}), bf16[32,48,384]{2,1,0:T(8,128)(2,1)S(1)}, u32[]{:S(2)}, u32[]{:S(2)}) async-start(bf16[32,48,384]{2,1,0:T(8,128)(2,1)} %route.1), calls=%async_computation | async-start | bytes 2359296 | tf_op jit(solution)/shard_map/all_to_all | solution.py:510
  13.5 1.8 %collective-permute-start.5 = (bf16[160,1280]{1,0:T(8,128)(2,1)S(1)}, bf16[160,1280]{1,0:T(8,128)(2,1)S(1)}, u32[]{:S(2)}, u32[]{:S(2)}) collective-permute-start(bf16[160,1280]{1,0:T(8,128)(2,1)S(1)} %constant_dynamic-update-slice_fusion.refs_0_), channel_id=1, source_target_pairs={{0,48},{8,200},{16,0},{24,216},{32,16},{40,232},{48,32},{56,248},{... | collective-permute-start | bytes 1228808 | tf_op jit(solution)/shard_map/ppermute | solution.py:60
  15.3 1.8 %collective-permute-start.6 = (bf16[160,1280]{1,0:T(8,128)(2,1)S(1)}, bf16[160,1280]{1,0:T(8,128)(2,1)S(1)}, u32[]{:S(2)}, u32[]{:S(2)}) collective-permute-start(bf16[160,1280]{1,0:T(8,128)(2,1)S(1)} %constant_dynamic-update-slice_fusion.refs_0_), channel_id=1, source_target_pairs={{0,32},{8,136},{16,48},{24,152},{32,0},{40,168},{48,16},{56,184},{... | collective-permute-start | bytes 1228808 | tf_op jit(solution)/shard_map/ppermute | solution.py:60
  17.2 11.1 %all-to-all-done.arrived = bf16[32,48,384]{2,1,0:T(8,128)(2,1)S(1)} async-done(((bf16[32,48,384]{2,1,0:T(8,128)(2,1)}), bf16[32,48,384]{2,1,0:T(8,128)(2,1)S(1)}, u32[]{:S(2)}, u32[]{:S(2)}) %all-to-all-start) | async-done | bytes 1179680 | tf_op jit(solution)/shard_map/all_to_all | solution.py:510
  28.2 1.6 %place.1.refs_2_ = bf16[320,768]{1,0:T(8,128)(2,1)S(1)} custom-call(bf16[32,48,384]{2,1,0:T(8,128)(2,1)S(1)} %all-to-all-done.arrived), custom_call_target="tpu_custom_call" | custom-call | tf_op jit(solution)/shard_map/place/pallas_call | solution.py:137
  29.8 5.9 %collective-permute-start.2 = (bf16[320,768]{1,0:T(8,128)(2,1)S(1)}, bf16[320,768]{1,0:T(8,128)(2,1)S(1)}, u32[]{:S(2)}, u32[]{:S(2)}) collective-permute-start(bf16[320,768]{1,0:T(8,128)(2,1)S(1)} %place.1.refs_2_), channel_id=1, source_target_pairs={{0,7},{1,0},{2,1},{3,2},{4,3},{5,4},{6,5},{7,6},{8,15},{9,8},{10,9... | collective-permute-start | bytes 1474568 | tf_op jit(solution)/shard_map/ppermute | solution.py:50
  35.8 2.0 %collective-permute-done.6.refs_3_ = bf16[160,1280]{1,0:T(8,128)(2,1)S(1)} collective-permute-done((bf16[160,1280]{1,0:T(8,128)(2,1)S(1)}, bf16[160,1280]{1,0:T(8,128)(2,1)S(1)}, u32[]{:S(2)}, u32[]{:S(2)}) %collective-permute-start.6) | collective-permute-done | bytes 409632 | tf_op jit(solution)/shard_map/ppermute | solution.py:60
  39.0 1.6 %collective-permute-start.11 = (bf16[640,1280]{1,0:T(8,128)(2,1)S(1)}, bf16[640,1280]{1,0:T(8,128)(2,1)S(1)}, u32[]{:S(2)}, u32[]{:S(2)}) collective-permute-start(bf16[640,1280]{1,0:T(8,128)(2,1)S(1)} %join.1.refs_5_.refs_2_), channel_id=1, source_target_pairs={{0,128},{8,40},{16,144},{24,56},{32,160},{40,8},{48,176},{56,24},{... | collective-permute-start | bytes 4915208 | tf_op jit(solution)/shard_map/ppermute | solution.py:60
  40.6 2.0 %collective-permute-start.9 = (bf16[640,1280]{1,0:T(8,128)(2,1)S(1)}, bf16[640,1280]{1,0:T(8,128)(2,1)S(1)}, u32[]{:S(2)}, u32[]{:S(2)}) collective-permute-start(bf16[640,1280]{1,0:T(8,128)(2,1)S(1)} %join.1.refs_5_.refs_2_), channel_id=1, source_target_pairs={{0,64},{8,24},{16,80},{24,40},{32,96},{40,56},{48,112},{56,8},{64,... | collective-permute-start | bytes 4915208 | tf_op jit(solution)/shard_map/ppermute | solution.py:60
  42.7 4.6 %collective-permute-done.2.refs_3_ = bf16[320,768]{1,0:T(8,128)(2,1)S(1)} collective-permute-done((bf16[320,768]{1,0:T(8,128)(2,1)S(1)}, bf16[320,768]{1,0:T(8,128)(2,1)S(1)}, u32[]{:S(2)}, u32[]{:S(2)}) %collective-permute-start.2) | collective-permute-done | bytes 491552 | tf_op jit(solution)/shard_map/ppermute | solution.py:50
  47.3 3.7 %collective-permute-start.3 = (bf16[320,768]{1,0:T(8,128)(2,1)S(1)}, bf16[320,768]{1,0:T(8,128)(2,1)S(1)}, u32[]{:S(2)}, u32[]{:S(2)}) collective-permute-start(bf16[320,768]{1,0:T(8,128)(2,1)S(1)} %collective-permute-done.2.refs_3_), channel_id=1, source_target_pairs={{0,7},{1,0},{2,1},{3,2},{4,3},{5,4},{6,5},{7,6},{8,15},{9,8},{10,9... | collective-permute-start | bytes 1474568 | tf_op jit(solution)/shard_map/ppermute | solution.py:50
  51.0 10.7 %collective-permute-done.3.refs_4_ = bf16[320,768]{1,0:T(8,128)(2,1)S(1)} collective-permute-done((bf16[320,768]{1,0:T(8,128)(2,1)S(1)}, bf16[320,768]{1,0:T(8,128)(2,1)S(1)}, u32[]{:S(2)}, u32[]{:S(2)}) %collective-permute-start.3) | collective-permute-done | bytes 491552 | tf_op jit(solution)/shard_map/ppermute | solution.py:50
  61.7 3.7 %collective-permute-start.7 = (bf16[320,768]{1,0:T(8,128)(2,1)S(1)}, bf16[320,768]{1,0:T(8,128)(2,1)S(1)}, u32[]{:S(2)}, u32[]{:S(2)}) collective-permute-start(bf16[320,768]{1,0:T(8,128)(2,1)S(1)} %collective-permute-done.3.refs_4_), channel_id=1, source_target_pairs={{0,7},{1,0},{2,1},{3,2},{4,3},{5,4},{6,5},{7,6},{8,15},{9,8},{10,9... | collective-permute-start | bytes 1474568 | tf_op jit(solution)/shard_map/ppermute | solution.py:50
  65.4 3.1 %project.1 = (f32[384,1280]{1,0:T(8,128)S(1)}, f32[384,1280]{1,0:T(8,128)S(1)}, bf16[320,1280]{1,0:T(8,128)(2,1)S(1)}, f32[384,128]{1,0:T(8,128)S(1)}, bf16[1600,768]{1,0:T(8,128)(2,1)S(1)}) custom-call(s32[16]{0:T(128)S(1)} %concatenate.6.where.small, bf16[32,48,384]{2,1,0:T(8,128)(2,1)S(1)} %all-to-all-done.arrived, ...), custom_call_target="tpu_custom_call" | custom-call | tf_op jit(solution)/shard_map/project/pallas_call | solution.py:254
  68.5 6.7 %collective-permute-done.7.refs_0_ = bf16[320,768]{1,0:T(8,128)(2,1)S(1)} collective-permute-done((bf16[320,768]{1,0:T(8,128)(2,1)S(1)}, bf16[320,768]{1,0:T(8,128)(2,1)S(1)}, u32[]{:S(2)}, u32[]{:S(2)}) %collective-permute-start.7) | collective-permute-done | bytes 491552 | tf_op jit(solution)/shard_map/ppermute | solution.py:50
  75.2 3.4 %collective-permute-done.8.refs_1_ = bf16[320,768]{1,0:T(8,128)(2,1)S(1)} collective-permute-done((bf16[320,768]{1,0:T(8,128)(2,1)S(1)}, bf16[320,768]{1,0:T(8,128)(2,1)S(1)}, u32[]{:S(2)}, u32[]{:S(2)}) %collective-permute-start.8) | collective-permute-done | bytes 491552 | tf_op jit(solution)/shard_map/ppermute | solution.py:50
  78.8 3.3 %collective-permute-start.13 = (bf16[160,768]{1,0:T(8,128)(2,1)S(1)}, bf16[160,768]{1,0:T(8,128)(2,1)S(1)}, u32[]{:S(2)}, u32[]{:S(2)}) collective-permute-start(bf16[160,768]{1,0:T(8,128)(2,1)S(1)} %slice.7), channel_id=1, source_target_pairs={{0,7},{1,0},{2,1},{3,2},{4,3},{5,4},{6,5},{7,6},{8,15},{9,8},{10,9... | collective-permute-start | bytes 737288 | tf_op jit(solution)/shard_map/ppermute | solution.py:50
  82.1 2.4 %far.1 = (f32[384,1280]{1,0:T(8,128)S(1)}, f32[384,1280]{1,0:T(8,128)S(1)}, bf16[640,768]{1,0:T(8,128)(2,1)S(1)}) custom-call(s32[16]{0:T(128)S(1)} %concatenate.6.where.small, f32[384,1280]{1,0:T(8,128)S(1)} %get-tuple-element.42.own, f32[384,1280]{1,0:T(8,128)S(1)} %get-tuple-element.43.other, bf16[320,768]{1,0:T(8,128)(2,1)S(1)} %collective-permute-done.7.refs_0_, ...), custom_call_target="tpu_custom_call" | custom-call | tf_op jit(solution)/shard_map/far/pallas_call | solution.py:288
  84.5 3.7 %across_other.1 = (f32[384,1280]{1,0:T(8,128)S(1)}, bf16[320,1280]{1,0:T(8,128)(2,1)S(1)}) custom-call(s32[16]{0:T(128)S(1)} %concatenate.6.where.small, f32[384,1280]{1,0:T(8,128)S(1)} %get-tuple-element.45.other, bf16[320,1280]{1,0:T(8,128)(2,1)S(1)} %get-tuple-element.46.late, bf16[1600,768]{1,0:T(8,128)(2,1)S(1)} %get-tuple-element.40.whole, ...), custom_call_target="tpu_custom_call" | custom-call | tf_op jit(solution)/shard_map/across_other/pallas_call | solution.py:316
  89.3 3.7 %across_own.1.own = f32[384,1280]{1,0:T(8,128)S(1)} custom-call(s32[16]{0:T(128)S(1)} %concatenate.6.where.small, f32[384,1280]{1,0:T(8,128)S(1)} %get-tuple-element.52.own, bf16[320,1280]{1,0:T(8,128)(2,1)S(1)} %get-tuple-element.48.late, bf16[1600,768]{1,0:T(8,128)(2,1)S(1)} %get-tuple-element.40.whole, bf16[640,768]{1,0:T(8,128)(2,1)S(1)} %get-tuple-element.44.far, ...), custom_call_target="tpu_custom_call" | custom-call | tf_op jit(solution)/shard_map/across_own/pallas_call | solution.py:347
  93.2 4.6 %attention.1.own = bf16[384,640]{1,0:T(8,128)(2,1)S(1)} custom-call(s32[16]{0:T(128)S(1)} %concatenate.6.where.small, f32[384,1280]{1,0:T(8,128)S(1)} %across_own.1.own, f32[384,1280]{1,0:T(8,128)S(1)} %collective-permute-done.14.received, bf16[384,384]{1,0:T(8,128)(2,1)S(1)} %bitcast.8, f32[384,128]{1,0:T(8,128)S(1)} %get-tuple-element.54.advantage), custom_call_target="tpu_custom_call" | custom-call | tf_op jit(solution)/shard_map/attention/pallas_call | solution.py:418
  98.2 1.6 %collective-permute-done.15.other = bf16[384,640]{1,0:T(8,128)(2,1)S(1)} collective-permute-done((bf16[384,640]{1,0:T(8,128)(2,1)S(1)}, bf16[384,640]{1,0:T(8,128)(2,1)S(1)}, u32[]{:S(2)}, u32[]{:S(2)}) %collective-permute-start.15) | collective-permute-done | bytes 491552 | tf_op jit(solution)/shard_map/ppermute | solution.py:542
  99.8 1.6 %gradient.7 = bf16[640,640]{1,0:T(8,128)(2,1)S(1)} custom-call(s32[16]{0:T(128)S(1)} %concatenate.6.where.small, bf16[1600,768]{1,0:T(8,128)(2,1)S(1)} %get-tuple-element.40.whole, bf16[640,768]{1,0:T(8,128)(2,1)S(1)} %get-tuple-element.44.far, bf16[320,768]{1,0:T(8,128)(2,1)S(1)} %get-tuple-element.51.last, bf16[384,640]{1,0:T(8,128)(2,1)S(1)} %attention.1.own, ...), custom_call_target="tpu_custom_call" | custom-call | tf_op jit(solution)/shard_map/gradient/pallas_call | solution.py:446
  101.5 1.6 %gradient.6 = bf16[640,640]{1,0:T(8,128)(2,1)S(1)} custom-call(s32[16]{0:T(128)S(1)} %concatenate.6.where.small, bf16[1600,768]{1,0:T(8,128)(2,1)S(1)} %get-tuple-element.40.whole, bf16[640,768]{1,0:T(8,128)(2,1)S(1)} %get-tuple-element.44.far, bf16[320,768]{1,0:T(8,128)(2,1)S(1)} %get-tuple-element.51.last, bf16[384,640]{1,0:T(8,128)(2,1)S(1)} %attention.1.own, ...), custom_call_target="tpu_custom_call" | custom-call | tf_op jit(solution)/shard_map/gradient/pallas_call | solution.py:446
  103.1 3.1 %collective-permute-start.17 = (bf16[640,640]{1,0:T(8,128)(2,1)S(1)}, bf16[640,640]{1,0:T(8,128)(2,1)S(1)}, u32[]{:S(2)}, u32[]{:S(2)}) collective-permute-start(bf16[640,640]{1,0:T(8,128)(2,1)S(1)} %gradient.6), channel_id=1, source_target_pairs={{0,16},{8,72},{16,32},{24,88},{32,48},{40,104},{48,0},{56,120},{64... | collective-permute-start | bytes 2457608 | tf_op jit(solution)/shard_map/ppermute | solution.py:60
  106.3 1.6 %gradient.5 = bf16[640,640]{1,0:T(8,128)(2,1)S(1)} custom-call(s32[16]{0:T(128)S(1)} %concatenate.6.where.small, bf16[1600,768]{1,0:T(8,128)(2,1)S(1)} %get-tuple-element.40.whole, bf16[640,768]{1,0:T(8,128)(2,1)S(1)} %get-tuple-element.44.far, bf16[320,768]{1,0:T(8,128)(2,1)S(1)} %get-tuple-element.51.last, bf16[384,640]{1,0:T(8,128)(2,1)S(1)} %attention.1.own, ...), custom_call_target="tpu_custom_call" | custom-call | tf_op jit(solution)/shard_map/gradient/pallas_call | solution.py:446
  108.8 1.6 %gradient.4.own = bf16[640,640]{1,0:T(8,128)(2,1)S(1)} custom-call(s32[16]{0:T(128)S(1)} %concatenate.6.where.small, bf16[1600,768]{1,0:T(8,128)(2,1)S(1)} %get-tuple-element.40.whole, bf16[640,768]{1,0:T(8,128)(2,1)S(1)} %get-tuple-element.44.far, bf16[320,768]{1,0:T(8,128)(2,1)S(1)} %get-tuple-element.51.last, bf16[384,640]{1,0:T(8,128)(2,1)S(1)} %attention.1.own, ...), custom_call_target="tpu_custom_call" | custom-call | tf_op jit(solution)/shard_map/gradient/pallas_call | solution.py:446
  110.4 5.0 %collective-permute-done.18.refs_2_ = bf16[640,640]{1,0:T(8,128)(2,1)S(1)} collective-permute-done((bf16[640,640]{1,0:T(8,128)(2,1)S(1)}, bf16[640,640]{1,0:T(8,128)(2,1)S(1)}, u32[]{:S(2)}, u32[]{:S(2)}) %collective-permute-start.18) | collective-permute-done | bytes 819232 | tf_op jit(solution)/shard_map/ppermute | solution.py:60
  115.5 8.7 %collective-permute-done.17.refs_1_ = bf16[640,640]{1,0:T(8,128)(2,1)S(1)} collective-permute-done((bf16[640,640]{1,0:T(8,128)(2,1)S(1)}, bf16[640,640]{1,0:T(8,128)(2,1)S(1)}, u32[]{:S(2)}, u32[]{:S(2)}) %collective-permute-start.17) | collective-permute-done | bytes 819232 | tf_op jit(solution)/shard_map/ppermute | solution.py:60
  127.6 3.3 %collective-permute-done.19.first = bf16[160,640]{1,0:T(8,128)(2,1)S(1)} collective-permute-done((bf16[160,640]{1,0:T(8,128)(2,1)S(1)}, bf16[160,640]{1,0:T(8,128)(2,1)S(1)}, u32[]{:S(2)}, u32[]{:S(2)}) %collective-permute-start.19) | collective-permute-done | bytes 204832 | tf_op jit(solution)/shard_map/ppermute | solution.py:60
  131.8 2.6 %collective-permute-done.21.third = bf16[160,640]{1,0:T(8,128)(2,1)S(1)} collective-permute-done((bf16[160,640]{1,0:T(8,128)(2,1)S(1)}, bf16[160,640]{1,0:T(8,128)(2,1)S(1)}, u32[]{:S(2)}, u32[]{:S(2)}) %collective-permute-start.21) | collective-permute-done | bytes 204832 | tf_op jit(solution)/shard_map/ppermute | solution.py:60
  (46 shorter events, 11.0 us)
Async XLA Ops:
  0.0 11.9 %copy-start.1 = (bf16[160,1,640]{2,0,1:T(8,128)(2,1)S(1)}, bf16[160,1,640]{2,0,1:T(8,128)(2,1)}, u32[]{:S(2)}) copy-start(bf16[160,1,640]{2,0,1:T(8,128)(2,1)} %param.15) | copy-start | bytes 614404
  0.0 12.0 %copy-start.2 = (bf16[160,1,640]{2,0,1:T(8,128)(2,1)S(1)}, bf16[160,1,640]{2,0,1:T(8,128)(2,1)}, u32[]{:S(2)}) copy-start(bf16[160,1,640]{2,0,1:T(8,128)(2,1)} %param.16) | copy-start | bytes 614404
  4.2 12.9 %copy-start.3 = (s32[4]{0:T(128)S(1)}, s32[4]{0:T(128)}, u32[]{:S(2)}) copy-start(s32[4]{0:T(128)} %rewards.1) | copy-start | bytes 52
  4.2 12.9 %copy-start.4 = (s32[4]{0:T(128)S(1)}, s32[4]{0:T(128)}, u32[]{:S(2)}) copy-start(s32[4]{0:T(128)} %groups.1) | copy-start | bytes 52
  4.2 12.9 %copy-start.5 = (s32[1,4]{1,0:T(1,128)S(1)}, s32[1,4]{1,0:T(1,128)}, u32[]{:S(2)}) copy-start(s32[1,4]{1,0:T(1,128)} %param.12) | copy-start | bytes 52
  4.2 24.0 %all-to-all-start = ((bf16[32,48,384]{2,1,0:T(8,128)(2,1)}), bf16[32,48,384]{2,1,0:T(8,128)(2,1)S(1)}, u32[]{:S(2)}, u32[]{:S(2)}) async-start(bf16[32,48,384]{2,1,0:T(8,128)(2,1)} %route.1), calls=%async_computation | async-start | bytes 2359296 | tf_op jit(solution)/shard_map/all_to_all | solution.py:510
  12.0 23.8 %collective-permute-start.4 = (bf16[160,1280]{1,0:T(8,128)(2,1)S(1)}, bf16[160,1280]{1,0:T(8,128)(2,1)S(1)}, u32[]{:S(2)}, u32[]{:S(2)}) collective-permute-start(bf16[160,1280]{1,0:T(8,128)(2,1)S(1)} %constant_dynamic-update-slice_fusion.refs_0_), channel_id=1, source_target_pairs={{0,16},{8,72},{16,32},{24,88},{32,48},{40,104},{48,0},{56,120},{64... | collective-permute-start | bytes 1228808 | tf_op jit(solution)/shard_map/ppermute | solution.py:60
  13.5 22.2 %collective-permute-start.5 = (bf16[160,1280]{1,0:T(8,128)(2,1)S(1)}, bf16[160,1280]{1,0:T(8,128)(2,1)S(1)}, u32[]{:S(2)}, u32[]{:S(2)}) collective-permute-start(bf16[160,1280]{1,0:T(8,128)(2,1)S(1)} %constant_dynamic-update-slice_fusion.refs_0_), channel_id=1, source_target_pairs={{0,48},{8,200},{16,0},{24,216},{32,16},{40,232},{48,32},{56,248},{... | collective-permute-start | bytes 1228808 | tf_op jit(solution)/shard_map/ppermute | solution.py:60
  15.3 22.5 %collective-permute-start.6 = (bf16[160,1280]{1,0:T(8,128)(2,1)S(1)}, bf16[160,1280]{1,0:T(8,128)(2,1)S(1)}, u32[]{:S(2)}, u32[]{:S(2)}) collective-permute-start(bf16[160,1280]{1,0:T(8,128)(2,1)S(1)} %constant_dynamic-update-slice_fusion.refs_0_), channel_id=1, source_target_pairs={{0,32},{8,136},{16,48},{24,152},{32,0},{40,168},{48,16},{56,184},{... | collective-permute-start | bytes 1228808 | tf_op jit(solution)/shard_map/ppermute | solution.py:60
  29.8 17.5 %collective-permute-start.2 = (bf16[320,768]{1,0:T(8,128)(2,1)S(1)}, bf16[320,768]{1,0:T(8,128)(2,1)S(1)}, u32[]{:S(2)}, u32[]{:S(2)}) collective-permute-start(bf16[320,768]{1,0:T(8,128)(2,1)S(1)} %place.1.refs_2_), channel_id=1, source_target_pairs={{0,7},{1,0},{2,1},{3,2},{4,3},{5,4},{6,5},{7,6},{8,15},{9,8},{10,9... | collective-permute-start | bytes 1474568 | tf_op jit(solution)/shard_map/ppermute | solution.py:50
  35.8 15.2 %collective-permute-start = (bf16[320,768]{1,0:T(8,128)(2,1)S(1)}, bf16[320,768]{1,0:T(8,128)(2,1)S(1)}, u32[]{:S(2)}, u32[]{:S(2)}) collective-permute-start(bf16[320,768]{1,0:T(8,128)(2,1)S(1)} %place.1.refs_2_), channel_id=1, source_target_pairs={{0,1},{1,2},{2,3},{3,4},{4,5},{5,6},{6,7},{7,0},{8,9},{9,10},{10,1... | collective-permute-start | bytes 1474568 | tf_op jit(solution)/shard_map/ppermute | solution.py:50
  37.9 46.6 %collective-permute-start.10 = (bf16[640,1280]{1,0:T(8,128)(2,1)S(1)}, bf16[640,1280]{1,0:T(8,128)(2,1)S(1)}, u32[]{:S(2)}, u32[]{:S(2)}) collective-permute-start(bf16[640,1280]{1,0:T(8,128)(2,1)S(1)} %join.1.refs_5_.refs_2_), channel_id=1, source_target_pairs={{0,192},{8,56},{16,208},{24,8},{32,224},{40,24},{48,240},{56,40},{... | collective-permute-start | bytes 4915208 | tf_op jit(solution)/shard_map/ppermute | solution.py:60
  39.0 45.5 %collective-permute-start.11 = (bf16[640,1280]{1,0:T(8,128)(2,1)S(1)}, bf16[640,1280]{1,0:T(8,128)(2,1)S(1)}, u32[]{:S(2)}, u32[]{:S(2)}) collective-permute-start(bf16[640,1280]{1,0:T(8,128)(2,1)S(1)} %join.1.refs_5_.refs_2_), channel_id=1, source_target_pairs={{0,128},{8,40},{16,144},{24,56},{32,160},{40,8},{48,176},{56,24},{... | collective-permute-start | bytes 4915208 | tf_op jit(solution)/shard_map/ppermute | solution.py:60
  40.6 43.8 %collective-permute-start.9 = (bf16[640,1280]{1,0:T(8,128)(2,1)S(1)}, bf16[640,1280]{1,0:T(8,128)(2,1)S(1)}, u32[]{:S(2)}, u32[]{:S(2)}) collective-permute-start(bf16[640,1280]{1,0:T(8,128)(2,1)S(1)} %join.1.refs_5_.refs_2_), channel_id=1, source_target_pairs={{0,64},{8,24},{16,80},{24,40},{32,96},{40,56},{48,112},{56,8},{64,... | collective-permute-start | bytes 4915208 | tf_op jit(solution)/shard_map/ppermute | solution.py:60
  47.3 14.4 %collective-permute-start.3 = (bf16[320,768]{1,0:T(8,128)(2,1)S(1)}, bf16[320,768]{1,0:T(8,128)(2,1)S(1)}, u32[]{:S(2)}, u32[]{:S(2)}) collective-permute-start(bf16[320,768]{1,0:T(8,128)(2,1)S(1)} %collective-permute-done.2.refs_3_), channel_id=1, source_target_pairs={{0,7},{1,0},{2,1},{3,2},{4,3},{5,4},{6,5},{7,6},{8,15},{9,8},{10,9... | collective-permute-start | bytes 1474568 | tf_op jit(solution)/shard_map/ppermute | solution.py:50
  51.0 14.4 %collective-permute-start.1 = (bf16[320,768]{1,0:T(8,128)(2,1)S(1)}, bf16[320,768]{1,0:T(8,128)(2,1)S(1)}, u32[]{:S(2)}, u32[]{:S(2)}) collective-permute-start(bf16[320,768]{1,0:T(8,128)(2,1)S(1)} %collective-permute-done.refs_1_), channel_id=1, source_target_pairs={{0,1},{1,2},{2,3},{3,4},{4,5},{5,6},{6,7},{7,0},{8,9},{9,10},{10,1... | collective-permute-start | bytes 1474568 | tf_op jit(solution)/shard_map/ppermute | solution.py:50
  61.7 13.5 %collective-permute-start.7 = (bf16[320,768]{1,0:T(8,128)(2,1)S(1)}, bf16[320,768]{1,0:T(8,128)(2,1)S(1)}, u32[]{:S(2)}, u32[]{:S(2)}) collective-permute-start(bf16[320,768]{1,0:T(8,128)(2,1)S(1)} %collective-permute-done.3.refs_4_), channel_id=1, source_target_pairs={{0,7},{1,0},{2,1},{3,2},{4,3},{5,4},{6,5},{7,6},{8,15},{9,8},{10,9... | collective-permute-start | bytes 1474568 | tf_op jit(solution)/shard_map/ppermute | solution.py:50
  65.4 13.3 %collective-permute-start.8 = (bf16[320,768]{1,0:T(8,128)(2,1)S(1)}, bf16[320,768]{1,0:T(8,128)(2,1)S(1)}, u32[]{:S(2)}, u32[]{:S(2)}) collective-permute-start(bf16[320,768]{1,0:T(8,128)(2,1)S(1)} %collective-permute-done.1.refs_0_), channel_id=1, source_target_pairs={{0,1},{1,2},{2,3},{3,4},{4,5},{5,6},{6,7},{7,0},{8,9},{9,10},{10,1... | collective-permute-start | bytes 1474568 | tf_op jit(solution)/shard_map/ppermute | solution.py:50
  78.7 9.5 %collective-permute-start.12 = (bf16[160,768]{1,0:T(8,128)(2,1)S(1)}, bf16[160,768]{1,0:T(8,128)(2,1)S(1)}, u32[]{:S(2)}, u32[]{:S(2)}) collective-permute-start(bf16[160,768]{1,0:T(8,128)(2,1)S(1)} %slice.6), channel_id=1, source_target_pairs={{0,1},{1,2},{2,3},{3,4},{4,5},{5,6},{6,7},{7,0},{8,9},{9,10},{10,1... | collective-permute-start | bytes 737288 | tf_op jit(solution)/shard_map/ppermute | solution.py:50
  78.8 9.4 %collective-permute-start.13 = (bf16[160,768]{1,0:T(8,128)(2,1)S(1)}, bf16[160,768]{1,0:T(8,128)(2,1)S(1)}, u32[]{:S(2)}, u32[]{:S(2)}) collective-permute-start(bf16[160,768]{1,0:T(8,128)(2,1)S(1)} %slice.7), channel_id=1, source_target_pairs={{0,7},{1,0},{2,1},{3,2},{4,3},{5,4},{6,5},{7,6},{8,15},{9,8},{10,9... | collective-permute-start | bytes 737288 | tf_op jit(solution)/shard_map/ppermute | solution.py:50
  88.9 4.3 %collective-permute-start.14 = (f32[384,1280]{1,0:T(8,128)S(1)}, f32[384,1280]{1,0:T(8,128)S(1)}, u32[]{:S(2)}, u32[]{:S(2)}) collective-permute-start(f32[384,1280]{1,0:T(8,128)S(1)} %get-tuple-element.53), channel_id=1, source_target_pairs={{0,8},{8,0},{1,9},{9,1},{2,10},{10,2},{3,11},{11,3},{4,12},{12,4},... | collective-permute-start | bytes 5898248 | tf_op jit(solution)/shard_map/ppermute | solution.py:538
  89.3 4.0 %copy-start = (bf16[384,1,384]{2,0,1:T(8,128)(2,1)S(1)}, bf16[384,1,384]{2,0,1:T(8,128)(2,1)}, u32[]{:S(2)}) copy-start(bf16[384,1,384]{2,0,1:T(8,128)(2,1)} %param.17) | copy-start | bytes 884740
  97.9 2.0 %collective-permute-start.15 = (bf16[384,640]{1,0:T(8,128)(2,1)S(1)}, bf16[384,640]{1,0:T(8,128)(2,1)S(1)}, u32[]{:S(2)}, u32[]{:S(2)}) collective-permute-start(bf16[384,640]{1,0:T(8,128)(2,1)S(1)} %attention.1.own), channel_id=1, source_target_pairs={{0,8},{8,0},{1,9},{9,1},{2,10},{10,2},{3,11},{11,3},{4,12},{12,4},... | collective-permute-start | bytes 1474568 | tf_op jit(solution)/shard_map/ppermute | solution.py:542
  101.4 14.0 %collective-permute-start.18 = (bf16[640,640]{1,0:T(8,128)(2,1)S(1)}, bf16[640,640]{1,0:T(8,128)(2,1)S(1)}, u32[]{:S(2)}, u32[]{:S(2)}) collective-permute-start(bf16[640,640]{1,0:T(8,128)(2,1)S(1)} %gradient.7), channel_id=1, source_target_pairs={{0,32},{8,136},{16,48},{24,152},{32,0},{40,168},{48,16},{56,184},{... | collective-permute-start | bytes 2457608 | tf_op jit(solution)/shard_map/ppermute | solution.py:60
  103.1 21.0 %collective-permute-start.17 = (bf16[640,640]{1,0:T(8,128)(2,1)S(1)}, bf16[640,640]{1,0:T(8,128)(2,1)S(1)}, u32[]{:S(2)}, u32[]{:S(2)}) collective-permute-start(bf16[640,640]{1,0:T(8,128)(2,1)S(1)} %gradient.6), channel_id=1, source_target_pairs={{0,16},{8,72},{16,32},{24,88},{32,48},{40,104},{48,0},{56,120},{64... | collective-permute-start | bytes 2457608 | tf_op jit(solution)/shard_map/ppermute | solution.py:60
  107.9 16.2 %collective-permute-start.16 = (bf16[640,640]{1,0:T(8,128)(2,1)S(1)}, bf16[640,640]{1,0:T(8,128)(2,1)S(1)}, u32[]{:S(2)}, u32[]{:S(2)}) collective-permute-start(bf16[640,640]{1,0:T(8,128)(2,1)S(1)} %gradient.5), channel_id=1, source_target_pairs={{0,48},{8,200},{16,0},{24,216},{32,16},{40,232},{48,32},{56,248},{... | collective-permute-start | bytes 2457608 | tf_op jit(solution)/shard_map/ppermute | solution.py:60
  125.1 5.8 %collective-permute-start.19 = (bf16[160,640]{1,0:T(8,128)(2,1)S(1)}, bf16[160,640]{1,0:T(8,128)(2,1)S(1)}, u32[]{:S(2)}, u32[]{:S(2)}) collective-permute-start(bf16[160,640]{1,0:T(8,128)(2,1)S(1)} %get-tuple-element.56), channel_id=1, source_target_pairs={{0,64},{8,24},{16,80},{24,40},{32,96},{40,56},{48,112},{56,8},{64,... | collective-permute-start | bytes 614408 | tf_op jit(solution)/shard_map/ppermute | solution.py:60
  126.1 5.8 %collective-permute-start.20 = (bf16[160,640]{1,0:T(8,128)(2,1)S(1)}, bf16[160,640]{1,0:T(8,128)(2,1)S(1)}, u32[]{:S(2)}, u32[]{:S(2)}) collective-permute-start(bf16[160,640]{1,0:T(8,128)(2,1)S(1)} %get-tuple-element.57), channel_id=1, source_target_pairs={{0,192},{8,56},{16,208},{24,8},{32,224},{40,24},{48,240},{56,40},{... | collective-permute-start | bytes 614408 | tf_op jit(solution)/shard_map/ppermute | solution.py:60
  127.2 7.3 %collective-permute-start.21 = (bf16[160,640]{1,0:T(8,128)(2,1)S(1)}, bf16[160,640]{1,0:T(8,128)(2,1)S(1)}, u32[]{:S(2)}, u32[]{:S(2)}) collective-permute-start(bf16[160,640]{1,0:T(8,128)(2,1)S(1)} %get-tuple-element.58), channel_id=1, source_target_pairs={{0,128},{8,40},{16,144},{24,56},{32,160},{40,8},{48,176},{56,24},{... | collective-permute-start | bytes 614408 | tf_op jit(solution)/shard_map/ppermute | solution.py:60
where the time goes:
time: 136 us; the launch traced here: 135 us
  waiting for transfers between devices  61 us (45%)
  starting transfers between devices  41.5 us (31%)
  Pallas kernels  32.4 us (24%)
    ppermute x8, waiting for transfers between devices, shift(): lax.ppermute(value, axis, [(i, (i + by) % size) for i in range(size)])  25.5 us
    ppermute x12, waiting for transfers between devices, turned(): return lax.ppermute(value, ('y', 'x', 'c'), pairs)  22.6 us
    ppermute x8, starting transfers between devices, shift(): lax.ppermute(value, axis, [(i, (i + by) % size) for i in range(size)])  16.7 us
    ppermute x12, starting transfers between devices, turned(): return lax.ppermute(value, ('y', 'x', 'c'), pairs)  16.5 us
    all_to_all x1, waiting for transfers between devices, body(): lax.all_to_all(outgoing, ('y', 'x', 'c'), split_axis=0, concat_axis=0, ti...  11.1 us
    all_to_all x1, starting transfers between devices, body(): lax.all_to_all(outgoing, ('y', 'x', 'c'), split_axis=0, concat_axis=0, ti...  7.68 us
    pallas_call x4, Pallas kernels, gradient_part(): pl.pallas_call(kernel, out_shape=PART, in_specs=[SMEM] + [VMEM] * 5, out_...  6.44 us
    pallas_call x1, Pallas kernels, attention(): pl.pallas_call(attention_kernel, out_shape=jax.ShapeDtypeStruct((ROWS, CO...  4.63 us
  transfers between devices with their start and end apart: 23, of which 13 were waited for; matrix products, arithmetic and copies ran while one was open for 0% of the time, Pallas kernels for 14%

commit v1 on v0

--- a/solution.py
+++ b/solution.py
@@ -453,6 +453,45 @@
     )(where, whole, far, last, own, other)
 
 
+def early_gradient(where, whole, far, last, own, move):
+    def kernel(where, whole, far, last, own, out, other_rows):
+        parts = [(whole, 0), (far, 5 * HALF), (last, 7 * HALF)]
+        first, _, first_stride, second_stride = turned_place(where)
+        rows = []
+        for k in range(4):
+            chunk = wrapped(first + move, 4) * first_stride + k * second_stride
+            rows.append(chunk_rows(parts, slot_of(chunk, where[3])))
+        rows = jnp.concatenate(rows, axis=0)
+        other_rows[...] = rows[:, ROWS:]
+        out[...] = dot(rows[:, :ROWS], own[...])
+
+    return pl.pallas_call(
+        kernel,
+        out_shape=(
+            jax.ShapeDtypeStruct((4 * CHUNK, COLS), F32),
+            jax.ShapeDtypeStruct((4 * CHUNK, ROWS), BF16),
+        ),
+        in_specs=[SMEM] + [VMEM] * 4,
+        out_specs=(VMEM,) * 2,
+        compiler_params=PARAMS,
+        name="early",
+    )(where, whole, far, last, own)
+
+
+def rest_gradient(early, rows, other):
+    def kernel(early, rows, other, out):
+        out[...] = (early[...] + dot(rows[...], other[...])).astype(BF16)
+
+    return pl.pallas_call(
+        kernel,
+        out_shape=PART,
+        in_specs=[VMEM] * 3,
+        out_specs=VMEM,
+        compiler_params=PARAMS,
+        name="rest",
+    )(early, rows, other)
+
+
 def middle_kernel(where, own, *refs):
     pieces, outs = refs[:3], refs[3:]
     second = turned_place(where)[1]
@@ -540,10 +579,14 @@
     cotangent = upstream.reshape(ROWS, 3 * HEAD_WIDTH)
     grad = attention(small, own, received, cotangent, advantage)
     grad_other = lax.ppermute(grad, "c", swap)
+    early, early_rows = early_gradient(small, whole, far, last, grad, 2)
 
     parts = []
     for move in (-1, 1, 2, 0):
-        part = gradient_part(small, whole, far, last, grad, grad_other, move)
+        if move == 2:
+            part = rest_gradient(early, early_rows, grad_other)
+        else:
+            part = gradient_part(small, whole, far, last, grad, grad_other, move)
         parts.append(turned(part, True, move) if move else part)
     sums = middle_sums(small, parts[3], parts[:3])
     parts = [turned(part, False, move) for move, part in zip((1, -1, 2), sums[1:])]

time: 136 us -> 135 us (level)
    pallas_call x0 -> x2, Pallas kernels: none -> 1.98 us  [the longest x1 1.36 us: early_gradient(): pl.pallas_call(kernel, out_shape=(jax.ShapeDtypeStruct((4 * CHUNK, COLS),...]
    pallas_call x4 -> x3, Pallas kernels: 6.44 us -> 4.83 us  [gradient_part(): pl.pallas_call(kernel, out_shape=PART, in_specs=[SMEM] + [VMEM] * 5, out_...]
    ppermute x1, waiting for transfers between devices: 1.63 us -> 0.26 us  [body(): grad_other = lax.ppermute(grad, 'c', swap)]
  transfers between devices with their start and end apart: 23 -> 23, of which waited for: 13 -> 13; matrix products, arithmetic and copies ran while one was open for 0% -> 0% of each run, Pallas kernels for 14% -> 15%
where the time goes in v1:
time: 135 us; the launch traced here: 134 us
  waiting for transfers between devices  59.7 us (44%)
  starting transfers between devices  41.6 us (31%)
  Pallas kernels  32.7 us (24%)
    ppermute x8, waiting for transfers between devices, shift(): lax.ppermute(value, axis, [(i, (i + by) % size) for i in range(size)])  25.5 us
    ppermute x12, waiting for transfers between devices, turned(): return lax.ppermute(value, ('y', 'x', 'c'), pairs)  22.5 us
    ppermute x8, starting transfers between devices, shift(): lax.ppermute(value, axis, [(i, (i + by) % size) for i in range(size)])  16.7 us
    ppermute x12, starting transfers between devices, turned(): return lax.ppermute(value, ('y', 'x', 'c'), pairs)  16.6 us
    all_to_all x1, waiting for transfers between devices, body(): lax.all_to_all(outgoing, ('y', 'x', 'c'), split_axis=0, concat_axis=0, ti...  11.1 us
    all_to_all x1, starting transfers between devices, body(): lax.all_to_all(outgoing, ('y', 'x', 'c'), split_axis=0, concat_axis=0, ti...  7.68 us
    pallas_call x3, Pallas kernels, gradient_part(): pl.pallas_call(kernel, out_shape=PART, in_specs=[SMEM] + [VMEM] * 5, out_...  4.83 us
    pallas_call x1, Pallas kernels, attention(): pl.pallas_call(attention_kernel, out_shape=jax.ShapeDtypeStruct((ROWS, CO...  4.63 us
  transfers between devices with their start and end apart: 23, of which 13 were waited for; matrix products, arithmetic and copies ran while one was open for 0% of the time, Pallas kernels for 15%

profile of v1, /device:TPU:8, one launch (start us, length us, event | category | flops | bytes accessed | tf_op | source)
XLA Modules:
  0.0 134.4 jit_solution(12560788027443630169)
XLA Ops:
  0.0 4.2 %route.1 = bf16[32,48,384]{2,1,0:T(8,128)(2,1)} custom-call(s32[4]{0:T(128)} %rewards.1, s32[4]{0:T(128)} %groups.1, s32[384]{0:T(512)} %shard.1, s32[384]{0:T(512)} %offset.1, bf16[384,640]{1,0:T(8,128)(2,1)} %tokens.1), custom_call_target="tpu_custom_call" | custom-call | tf_op jit(solution)/shard_map/route/pallas_call | solution.py:115
  4.2 7.7 %all-to-all-start = ((bf16[32,48,384]{2,1,0:T(8,128)(2,1)}), bf16[32,48,384]{2,1,0:T(8,128)(2,1)S(1)}, u32[]{:S(2)}, u32[]{:S(2)}) async-start(bf16[32,48,384]{2,1,0:T(8,128)(2,1)} %route.1), calls=%async_computation | async-start | bytes 2359296 | tf_op jit(solution)/shard_map/all_to_all | solution.py:549
  12.0 1.5 %collective-permute-start.4 = (bf16[160,1280]{1,0:T(8,128)(2,1)S(1)}, bf16[160,1280]{1,0:T(8,128)(2,1)S(1)}, u32[]{:S(2)}, u32[]{:S(2)}) collective-permute-start(bf16[160,1280]{1,0:T(8,128)(2,1)S(1)} %constant_dynamic-update-slice_fusion.refs_0_), channel_id=1, source_target_pairs={{0,16},{8,72},{16,32},{24,88},{32,48},{40,104},{48,0},{56,120},{64... | collective-permute-start | bytes 1228808 | tf_op jit(solution)/shard_map/ppermute | solution.py:60
  13.5 1.8 %collective-permute-start.5 = (bf16[160,1280]{1,0:T(8,128)(2,1)S(1)}, bf16[160,1280]{1,0:T(8,128)(2,1)S(1)}, u32[]{:S(2)}, u32[]{:S(2)}) collective-permute-start(bf16[160,1280]{1,0:T(8,128)(2,1)S(1)} %constant_dynamic-update-slice_fusion.refs_0_), channel_id=1, source_target_pairs={{0,48},{8,200},{16,0},{24,216},{32,16},{40,232},{48,32},{56,248},{... | collective-permute-start | bytes 1228808 | tf_op jit(solution)/shard_map/ppermute | solution.py:60
  15.3 1.8 %collective-permute-start.6 = (bf16[160,1280]{1,0:T(8,128)(2,1)S(1)}, bf16[160,1280]{1,0:T(8,128)(2,1)S(1)}, u32[]{:S(2)}, u32[]{:S(2)}) collective-permute-start(bf16[160,1280]{1,0:T(8,128)(2,1)S(1)} %constant_dynamic-update-slice_fusion.refs_0_), channel_id=1, source_target_pairs={{0,32},{8,136},{16,48},{24,152},{32,0},{40,168},{48,16},{56,184},{... | collective-permute-start | bytes 1228808 | tf_op jit(solution)/shard_map/ppermute | solution.py:60
  17.2 11.1 %all-to-all-done.arrived = bf16[32,48,384]{2,1,0:T(8,128)(2,1)S(1)} async-done(((bf16[32,48,384]{2,1,0:T(8,128)(2,1)}), bf16[32,48,384]{2,1,0:T(8,128)(2,1)S(1)}, u32[]{:S(2)}, u32[]{:S(2)}) %all-to-all-start) | async-done | bytes 1179680 | tf_op jit(solution)/shard_map/all_to_all | solution.py:549
  28.2 1.6 %place.1.refs_2_ = bf16[320,768]{1,0:T(8,128)(2,1)S(1)} custom-call(bf16[32,48,384]{2,1,0:T(8,128)(2,1)S(1)} %all-to-all-done.arrived), custom_call_target="tpu_custom_call" | custom-call | tf_op jit(solution)/shard_map/place/pallas_call | solution.py:137
  29.8 5.9 %collective-permute-start.2 = (bf16[320,768]{1,0:T(8,128)(2,1)S(1)}, bf16[320,768]{1,0:T(8,128)(2,1)S(1)}, u32[]{:S(2)}, u32[]{:S(2)}) collective-permute-start(bf16[320,768]{1,0:T(8,128)(2,1)S(1)} %place.1.refs_2_), channel_id=1, source_target_pairs={{0,7},{1,0},{2,1},{3,2},{4,3},{5,4},{6,5},{7,6},{8,15},{9,8},{10,9... | collective-permute-start | bytes 1474568 | tf_op jit(solution)/shard_map/ppermute | solution.py:50
  35.8 2.0 %collective-permute-done.6.refs_3_ = bf16[160,1280]{1,0:T(8,128)(2,1)S(1)} collective-permute-done((bf16[160,1280]{1,0:T(8,128)(2,1)S(1)}, bf16[160,1280]{1,0:T(8,128)(2,1)S(1)}, u32[]{:S(2)}, u32[]{:S(2)}) %collective-permute-start.6) | collective-permute-done | bytes 409632 | tf_op jit(solution)/shard_map/ppermute | solution.py:60
  39.0 1.6 %collective-permute-start.11 = (bf16[640,1280]{1,0:T(8,128)(2,1)S(1)}, bf16[640,1280]{1,0:T(8,128)(2,1)S(1)}, u32[]{:S(2)}, u32[]{:S(2)}) collective-permute-start(bf16[640,1280]{1,0:T(8,128)(2,1)S(1)} %join.1.refs_5_.refs_2_), channel_id=1, source_target_pairs={{0,128},{8,40},{16,144},{24,56},{32,160},{40,8},{48,176},{56,24},{... | collective-permute-start | bytes 4915208 | tf_op jit(solution)/shard_map/ppermute | solution.py:60
  40.6 2.0 %collective-permute-start.9 = (bf16[640,1280]{1,0:T(8,128)(2,1)S(1)}, bf16[640,1280]{1,0:T(8,128)(2,1)S(1)}, u32[]{:S(2)}, u32[]{:S(2)}) collective-permute-start(bf16[640,1280]{1,0:T(8,128)(2,1)S(1)} %join.1.refs_5_.refs_2_), channel_id=1, source_target_pairs={{0,64},{8,24},{16,80},{24,40},{32,96},{40,56},{48,112},{56,8},{64,... | collective-permute-start | bytes 4915208 | tf_op jit(solution)/shard_map/ppermute | solution.py:60
  42.7 4.7 %collective-permute-done.2.refs_3_ = bf16[320,768]{1,0:T(8,128)(2,1)S(1)} collective-permute-done((bf16[320,768]{1,0:T(8,128)(2,1)S(1)}, bf16[320,768]{1,0:T(8,128)(2,1)S(1)}, u32[]{:S(2)}, u32[]{:S(2)}) %collective-permute-start.2) | collective-permute-done | bytes 491552 | tf_op jit(solution)/shard_map/ppermute | solution.py:50
  47.3 3.7 %collective-permute-start.3 = (bf16[320,768]{1,0:T(8,128)(2,1)S(1)}, bf16[320,768]{1,0:T(8,128)(2,1)S(1)}, u32[]{:S(2)}, u32[]{:S(2)}) collective-permute-start(bf16[320,768]{1,0:T(8,128)(2,1)S(1)} %collective-permute-done.2.refs_3_), channel_id=1, source_target_pairs={{0,7},{1,0},{2,1},{3,2},{4,3},{5,4},{6,5},{7,6},{8,15},{9,8},{10,9... | collective-permute-start | bytes 1474568 | tf_op jit(solution)/shard_map/ppermute | solution.py:50
  51.0 10.7 %collective-permute-done.3.refs_4_ = bf16[320,768]{1,0:T(8,128)(2,1)S(1)} collective-permute-done((bf16[320,768]{1,0:T(8,128)(2,1)S(1)}, bf16[320,768]{1,0:T(8,128)(2,1)S(1)}, u32[]{:S(2)}, u32[]{:S(2)}) %collective-permute-start.3) | collective-permute-done | bytes 491552 | tf_op jit(solution)/shard_map/ppermute | solution.py:50
  61.7 3.7 %collective-permute-start.7 = (bf16[320,768]{1,0:T(8,128)(2,1)S(1)}, bf16[320,768]{1,0:T(8,128)(2,1)S(1)}, u32[]{:S(2)}, u32[]{:S(2)}) collective-permute-start(bf16[320,768]{1,0:T(8,128)(2,1)S(1)} %collective-permute-done.3.refs_4_), channel_id=1, source_target_pairs={{0,7},{1,0},{2,1},{3,2},{4,3},{5,4},{6,5},{7,6},{8,15},{9,8},{10,9... | collective-permute-start | bytes 1474568 | tf_op jit(solution)/shard_map/ppermute | solution.py:50
  65.4 3.1 %project.1 = (f32[384,1280]{1,0:T(8,128)S(1)}, f32[384,1280]{1,0:T(8,128)S(1)}, bf16[320,1280]{1,0:T(8,128)(2,1)S(1)}, f32[384,128]{1,0:T(8,128)S(1)}, bf16[1600,768]{1,0:T(8,128)(2,1)S(1)}) custom-call(s32[16]{0:T(128)S(1)} %concatenate.6.where.small, bf16[32,48,384]{2,1,0:T(8,128)(2,1)S(1)} %all-to-all-done.arrived, ...), custom_call_target="tpu_custom_call" | custom-call | tf_op jit(solution)/shard_map/project/pallas_call | solution.py:254
  68.5 6.8 %collective-permute-done.7.refs_0_ = bf16[320,768]{1,0:T(8,128)(2,1)S(1)} collective-permute-done((bf16[320,768]{1,0:T(8,128)(2,1)S(1)}, bf16[320,768]{1,0:T(8,128)(2,1)S(1)}, u32[]{:S(2)}, u32[]{:S(2)}) %collective-permute-start.7) | collective-permute-done | bytes 491552 | tf_op jit(solution)/shard_map/ppermute | solution.py:50
  75.3 3.4 %collective-permute-done.8.refs_1_ = bf16[320,768]{1,0:T(8,128)(2,1)S(1)} collective-permute-done((bf16[320,768]{1,0:T(8,128)(2,1)S(1)}, bf16[320,768]{1,0:T(8,128)(2,1)S(1)}, u32[]{:S(2)}, u32[]{:S(2)}) %collective-permute-start.8) | collective-permute-done | bytes 491552 | tf_op jit(solution)/shard_map/ppermute | solution.py:50
  78.8 3.3 %collective-permute-start.13 = (bf16[160,768]{1,0:T(8,128)(2,1)S(1)}, bf16[160,768]{1,0:T(8,128)(2,1)S(1)}, u32[]{:S(2)}, u32[]{:S(2)}) collective-permute-start(bf16[160,768]{1,0:T(8,128)(2,1)S(1)} %slice.7), channel_id=1, source_target_pairs={{0,7},{1,0},{2,1},{3,2},{4,3},{5,4},{6,5},{7,6},{8,15},{9,8},{10,9... | collective-permute-start | bytes 737288 | tf_op jit(solution)/shard_map/ppermute | solution.py:50
  82.1 2.4 %far.1 = (f32[384,1280]{1,0:T(8,128)S(1)}, f32[384,1280]{1,0:T(8,128)S(1)}, bf16[640,768]{1,0:T(8,128)(2,1)S(1)}) custom-call(s32[16]{0:T(128)S(1)} %concatenate.6.where.small, f32[384,1280]{1,0:T(8,128)S(1)} %get-tuple-element.44.own, f32[384,1280]{1,0:T(8,128)S(1)} %get-tuple-element.45.other, bf16[320,768]{1,0:T(8,128)(2,1)S(1)} %collective-permute-done.7.refs_0_, ...), custom_call_target="tpu_custom_call" | custom-call | tf_op jit(solution)/shard_map/far/pallas_call | solution.py:288
  84.5 3.7 %across_other.1 = (f32[384,1280]{1,0:T(8,128)S(1)}, bf16[320,1280]{1,0:T(8,128)(2,1)S(1)}) custom-call(s32[16]{0:T(128)S(1)} %concatenate.6.where.small, f32[384,1280]{1,0:T(8,128)S(1)} %get-tuple-element.47.other, bf16[320,1280]{1,0:T(8,128)(2,1)S(1)} %get-tuple-element.48.late, bf16[1600,768]{1,0:T(8,128)(2,1)S(1)} %get-tuple-element.42.whole, ...), custom_call_target="tpu_custom_call" | custom-call | tf_op jit(solution)/shard_map/across_other/pallas_call | solution.py:316
  89.3 3.7 %across_own.1.own = f32[384,1280]{1,0:T(8,128)S(1)} custom-call(s32[16]{0:T(128)S(1)} %concatenate.6.where.small, f32[384,1280]{1,0:T(8,128)S(1)} %get-tuple-element.54.own, bf16[320,1280]{1,0:T(8,128)(2,1)S(1)} %get-tuple-element.50.late, bf16[1600,768]{1,0:T(8,128)(2,1)S(1)} %get-tuple-element.42.whole, bf16[640,768]{1,0:T(8,128)(2,1)S(1)} %get-tuple-element.46.far, ...), custom_call_target="tpu_custom_call" | custom-call | tf_op jit(solution)/shard_map/across_own/pallas_call | solution.py:347
  93.3 4.6 %attention.1.own = bf16[384,640]{1,0:T(8,128)(2,1)S(1)} custom-call(s32[16]{0:T(128)S(1)} %concatenate.6.where.small, f32[384,1280]{1,0:T(8,128)S(1)} %across_own.1.own, f32[384,1280]{1,0:T(8,128)S(1)} %collective-permute-done.14.received, bf16[384,384]{1,0:T(8,128)(2,1)S(1)} %bitcast.8, f32[384,128]{1,0:T(8,128)S(1)} %get-tuple-element.56.advantage), custom_call_target="tpu_custom_call" | custom-call | tf_op jit(solution)/shard_map/attention/pallas_call | solution.py:418
  98.2 1.4 %early.1 = (f32[640,640]{1,0:T(8,128)S(1)}, bf16[640,384]{1,0:T(8,128)(2,1)S(1)}) custom-call(s32[16]{0:T(128)S(1)} %concatenate.6.where.small, bf16[1600,768]{1,0:T(8,128)(2,1)S(1)} %get-tuple-element.42.whole, bf16[640,768]{1,0:T(8,128)(2,1)S(1)} %get-tuple-element.46.far, bf16[320,768]{1,0:T(8,128)(2,1)S(1)} %get-tuple-element.53.last, ...), custom_call_target="tpu_custom_call" | custom-call | tf_op jit(solution)/shard_map/early/pallas_call | solution.py:468
  100.6 1.6 %gradient.5 = bf16[640,640]{1,0:T(8,128)(2,1)S(1)} custom-call(s32[16]{0:T(128)S(1)} %concatenate.6.where.small, bf16[1600,768]{1,0:T(8,128)(2,1)S(1)} %get-tuple-element.42.whole, bf16[640,768]{1,0:T(8,128)(2,1)S(1)} %get-tuple-element.46.far, bf16[320,768]{1,0:T(8,128)(2,1)S(1)} %get-tuple-element.53.last, bf16[384,640]{1,0:T(8,128)(2,1)S(1)} %attention.1.own, ...), custom_call_target="tpu_custom_call" | custom-call | tf_op jit(solution)/shard_map/gradient/pallas_call | solution.py:446
  102.2 3.1 %collective-permute-start.17 = (bf16[640,640]{1,0:T(8,128)(2,1)S(1)}, bf16[640,640]{1,0:T(8,128)(2,1)S(1)}, u32[]{:S(2)}, u32[]{:S(2)}) collective-permute-start(bf16[640,640]{1,0:T(8,128)(2,1)S(1)} %gradient.5), channel_id=1, source_target_pairs={{0,16},{8,72},{16,32},{24,88},{32,48},{40,104},{48,0},{56,120},{64... | collective-permute-start | bytes 2457608 | tf_op jit(solution)/shard_map/ppermute | solution.py:60
  105.3 1.6 %gradient.4 = bf16[640,640]{1,0:T(8,128)(2,1)S(1)} custom-call(s32[16]{0:T(128)S(1)} %concatenate.6.where.small, bf16[1600,768]{1,0:T(8,128)(2,1)S(1)} %get-tuple-element.42.whole, bf16[640,768]{1,0:T(8,128)(2,1)S(1)} %get-tuple-element.46.far, bf16[320,768]{1,0:T(8,128)(2,1)S(1)} %get-tuple-element.53.last, bf16[384,640]{1,0:T(8,128)(2,1)S(1)} %attention.1.own, ...), custom_call_target="tpu_custom_call" | custom-call | tf_op jit(solution)/shard_map/gradient/pallas_call | solution.py:446
  107.8 1.6 %gradient.3.own = bf16[640,640]{1,0:T(8,128)(2,1)S(1)} custom-call(s32[16]{0:T(128)S(1)} %concatenate.6.where.small, bf16[1600,768]{1,0:T(8,128)(2,1)S(1)} %get-tuple-element.42.whole, bf16[640,768]{1,0:T(8,128)(2,1)S(1)} %get-tuple-element.46.far, bf16[320,768]{1,0:T(8,128)(2,1)S(1)} %get-tuple-element.53.last, bf16[384,640]{1,0:T(8,128)(2,1)S(1)} %attention.1.own, ...), custom_call_target="tpu_custom_call" | custom-call | tf_op jit(solution)/shard_map/gradient/pallas_call | solution.py:446
  109.4 5.1 %collective-permute-done.18.refs_2_ = bf16[640,640]{1,0:T(8,128)(2,1)S(1)} collective-permute-done((bf16[640,640]{1,0:T(8,128)(2,1)S(1)}, bf16[640,640]{1,0:T(8,128)(2,1)S(1)}, u32[]{:S(2)}, u32[]{:S(2)}) %collective-permute-start.18) | collective-permute-done | bytes 819232 | tf_op jit(solution)/shard_map/ppermute | solution.py:60
  114.5 8.7 %collective-permute-done.17.refs_1_ = bf16[640,640]{1,0:T(8,128)(2,1)S(1)} collective-permute-done((bf16[640,640]{1,0:T(8,128)(2,1)S(1)}, bf16[640,640]{1,0:T(8,128)(2,1)S(1)}, u32[]{:S(2)}, u32[]{:S(2)}) %collective-permute-start.17) | collective-permute-done | bytes 819232 | tf_op jit(solution)/shard_map/ppermute | solution.py:60
  126.8 3.2 %collective-permute-done.19.first = bf16[160,640]{1,0:T(8,128)(2,1)S(1)} collective-permute-done((bf16[160,640]{1,0:T(8,128)(2,1)S(1)}, bf16[160,640]{1,0:T(8,128)(2,1)S(1)}, u32[]{:S(2)}, u32[]{:S(2)}) %collective-permute-start.19) | collective-permute-done | bytes 204832 | tf_op jit(solution)/shard_map/ppermute | solution.py:60
  131.0 2.5 %collective-permute-done.21.third = bf16[160,640]{1,0:T(8,128)(2,1)S(1)} collective-permute-done((bf16[160,640]{1,0:T(8,128)(2,1)S(1)}, bf16[160,640]{1,0:T(8,128)(2,1)S(1)}, u32[]{:S(2)}, u32[]{:S(2)}) %collective-permute-start.21) | collective-permute-done | bytes 204832 | tf_op jit(solution)/shard_map/ppermute | solution.py:60
  (47 shorter events, 10.6 us)
Async XLA Ops:
  0.0 11.9 %copy-start.1 = (bf16[160,1,640]{2,0,1:T(8,128)(2,1)S(1)}, bf16[160,1,640]{2,0,1:T(8,128)(2,1)}, u32[]{:S(2)}) copy-start(bf16[160,1,640]{2,0,1:T(8,128)(2,1)} %param.15) | copy-start | bytes 614404
  0.0 12.0 %copy-start.2 = (bf16[160,1,640]{2,0,1:T(8,128)(2,1)S(1)}, bf16[160,1,640]{2,0,1:T(8,128)(2,1)}, u32[]{:S(2)}) copy-start(bf16[160,1,640]{2,0,1:T(8,128)(2,1)} %param.16) | copy-start | bytes 614404
  4.2 12.9 %copy-start.3 = (s32[4]{0:T(128)S(1)}, s32[4]{0:T(128)}, u32[]{:S(2)}) copy-start(s32[4]{0:T(128)} %rewards.1) | copy-start | bytes 52
  4.2 12.9 %copy-start.4 = (s32[4]{0:T(128)S(1)}, s32[4]{0:T(128)}, u32[]{:S(2)}) copy-start(s32[4]{0:T(128)} %groups.1) | copy-start | bytes 52
  4.2 12.9 %copy-start.5 = (s32[1,4]{1,0:T(1,128)S(1)}, s32[1,4]{1,0:T(1,128)}, u32[]{:S(2)}) copy-start(s32[1,4]{1,0:T(1,128)} %param.12) | copy-start | bytes 52
  4.2 24.0 %all-to-all-start = ((bf16[32,48,384]{2,1,0:T(8,128)(2,1)}), bf16[32,48,384]{2,1,0:T(8,128)(2,1)S(1)}, u32[]{:S(2)}, u32[]{:S(2)}) async-start(bf16[32,48,384]{2,1,0:T(8,128)(2,1)} %route.1), calls=%async_computation | async-start | bytes 2359296 | tf_op jit(solution)/shard_map/all_to_all | solution.py:549
  12.0 23.8 %collective-permute-start.4 = (bf16[160,1280]{1,0:T(8,128)(2,1)S(1)}, bf16[160,1280]{1,0:T(8,128)(2,1)S(1)}, u32[]{:S(2)}, u32[]{:S(2)}) collective-permute-start(bf16[160,1280]{1,0:T(8,128)(2,1)S(1)} %constant_dynamic-update-slice_fusion.refs_0_), channel_id=1, source_target_pairs={{0,16},{8,72},{16,32},{24,88},{32,48},{40,104},{48,0},{56,120},{64... | collective-permute-start | bytes 1228808 | tf_op jit(solution)/shard_map/ppermute | solution.py:60
  13.5 22.2 %collective-permute-start.5 = (bf16[160,1280]{1,0:T(8,128)(2,1)S(1)}, bf16[160,1280]{1,0:T(8,128)(2,1)S(1)}, u32[]{:S(2)}, u32[]{:S(2)}) collective-permute-start(bf16[160,1280]{1,0:T(8,128)(2,1)S(1)} %constant_dynamic-update-slice_fusion.refs_0_), channel_id=1, source_target_pairs={{0,48},{8,200},{16,0},{24,216},{32,16},{40,232},{48,32},{56,248},{... | collective-permute-start | bytes 1228808 | tf_op jit(solution)/shard_map/ppermute | solution.py:60
  15.3 22.5 %collective-permute-start.6 = (bf16[160,1280]{1,0:T(8,128)(2,1)S(1)}, bf16[160,1280]{1,0:T(8,128)(2,1)S(1)}, u32[]{:S(2)}, u32[]{:S(2)}) collective-permute-start(bf16[160,1280]{1,0:T(8,128)(2,1)S(1)} %constant_dynamic-update-slice_fusion.refs_0_), channel_id=1, source_target_pairs={{0,32},{8,136},{16,48},{24,152},{32,0},{40,168},{48,16},{56,184},{... | collective-permute-start | bytes 1228808 | tf_op jit(solution)/shard_map/ppermute | solution.py:60
  29.8 17.5 %collective-permute-start.2 = (bf16[320,768]{1,0:T(8,128)(2,1)S(1)}, bf16[320,768]{1,0:T(8,128)(2,1)S(1)}, u32[]{:S(2)}, u32[]{:S(2)}) collective-permute-start(bf16[320,768]{1,0:T(8,128)(2,1)S(1)} %place.1.refs_2_), channel_id=1, source_target_pairs={{0,7},{1,0},{2,1},{3,2},{4,3},{5,4},{6,5},{7,6},{8,15},{9,8},{10,9... | collective-permute-start | bytes 1474568 | tf_op jit(solution)/shard_map/ppermute | solution.py:50
  35.8 15.3 %collective-permute-start = (bf16[320,768]{1,0:T(8,128)(2,1)S(1)}, bf16[320,768]{1,0:T(8,128)(2,1)S(1)}, u32[]{:S(2)}, u32[]{:S(2)}) collective-permute-start(bf16[320,768]{1,0:T(8,128)(2,1)S(1)} %place.1.refs_2_), channel_id=1, source_target_pairs={{0,1},{1,2},{2,3},{3,4},{4,5},{5,6},{6,7},{7,0},{8,9},{9,10},{10,1... | collective-permute-start | bytes 1474568 | tf_op jit(solution)/shard_map/ppermute | solution.py:50
  37.9 46.6 %collective-permute-start.10 = (bf16[640,1280]{1,0:T(8,128)(2,1)S(1)}, bf16[640,1280]{1,0:T(8,128)(2,1)S(1)}, u32[]{:S(2)}, u32[]{:S(2)}) collective-permute-start(bf16[640,1280]{1,0:T(8,128)(2,1)S(1)} %join.1.refs_5_.refs_2_), channel_id=1, source_target_pairs={{0,192},{8,56},{16,208},{24,8},{32,224},{40,24},{48,240},{56,40},{... | collective-permute-start | bytes 4915208 | tf_op jit(solution)/shard_map/ppermute | solution.py:60
  39.0 45.5 %collective-permute-start.11 = (bf16[640,1280]{1,0:T(8,128)(2,1)S(1)}, bf16[640,1280]{1,0:T(8,128)(2,1)S(1)}, u32[]{:S(2)}, u32[]{:S(2)}) collective-permute-start(bf16[640,1280]{1,0:T(8,128)(2,1)S(1)} %join.1.refs_5_.refs_2_), channel_id=1, source_target_pairs={{0,128},{8,40},{16,144},{24,56},{32,160},{40,8},{48,176},{56,24},{... | collective-permute-start | bytes 4915208 | tf_op jit(solution)/shard_map/ppermute | solution.py:60
  40.6 43.9 %collective-permute-start.9 = (bf16[640,1280]{1,0:T(8,128)(2,1)S(1)}, bf16[640,1280]{1,0:T(8,128)(2,1)S(1)}, u32[]{:S(2)}, u32[]{:S(2)}) collective-permute-start(bf16[640,1280]{1,0:T(8,128)(2,1)S(1)} %join.1.refs_5_.refs_2_), channel_id=1, source_target_pairs={{0,64},{8,24},{16,80},{24,40},{32,96},{40,56},{48,112},{56,8},{64,... | collective-permute-start | bytes 4915208 | tf_op jit(solution)/shard_map/ppermute | solution.py:60
  47.3 14.4 %collective-permute-start.3 = (bf16[320,768]{1,0:T(8,128)(2,1)S(1)}, bf16[320,768]{1,0:T(8,128)(2,1)S(1)}, u32[]{:S(2)}, u32[]{:S(2)}) collective-permute-start(bf16[320,768]{1,0:T(8,128)(2,1)S(1)} %collective-permute-done.2.refs_3_), channel_id=1, source_target_pairs={{0,7},{1,0},{2,1},{3,2},{4,3},{5,4},{6,5},{7,6},{8,15},{9,8},{10,9... | collective-permute-start | bytes 1474568 | tf_op jit(solution)/shard_map/ppermute | solution.py:50
  51.0 14.4 %collective-permute-start.1 = (bf16[320,768]{1,0:T(8,128)(2,1)S(1)}, bf16[320,768]{1,0:T(8,128)(2,1)S(1)}, u32[]{:S(2)}, u32[]{:S(2)}) collective-permute-start(bf16[320,768]{1,0:T(8,128)(2,1)S(1)} %collective-permute-done.refs_1_), channel_id=1, source_target_pairs={{0,1},{1,2},{2,3},{3,4},{4,5},{5,6},{6,7},{7,0},{8,9},{9,10},{10,1... | collective-permute-start | bytes 1474568 | tf_op jit(solution)/shard_map/ppermute | solution.py:50
  61.7 13.6 %collective-permute-start.7 = (bf16[320,768]{1,0:T(8,128)(2,1)S(1)}, bf16[320,768]{1,0:T(8,128)(2,1)S(1)}, u32[]{:S(2)}, u32[]{:S(2)}) collective-permute-start(bf16[320,768]{1,0:T(8,128)(2,1)S(1)} %collective-permute-done.3.refs_4_), channel_id=1, source_target_pairs={{0,7},{1,0},{2,1},{3,2},{4,3},{5,4},{6,5},{7,6},{8,15},{9,8},{10,9... | collective-permute-start | bytes 1474568 | tf_op jit(solution)/shard_map/ppermute | solution.py:50
  65.4 13.3 %collective-permute-start.8 = (bf16[320,768]{1,0:T(8,128)(2,1)S(1)}, bf16[320,768]{1,0:T(8,128)(2,1)S(1)}, u32[]{:S(2)}, u32[]{:S(2)}) collective-permute-start(bf16[320,768]{1,0:T(8,128)(2,1)S(1)} %collective-permute-done.1.refs_0_), channel_id=1, source_target_pairs={{0,1},{1,2},{2,3},{3,4},{4,5},{5,6},{6,7},{7,0},{8,9},{9,10},{10,1... | collective-permute-start | bytes 1474568 | tf_op jit(solution)/shard_map/ppermute | solution.py:50
  78.7 9.5 %collective-permute-start.12 = (bf16[160,768]{1,0:T(8,128)(2,1)S(1)}, bf16[160,768]{1,0:T(8,128)(2,1)S(1)}, u32[]{:S(2)}, u32[]{:S(2)}) collective-permute-start(bf16[160,768]{1,0:T(8,128)(2,1)S(1)} %slice.6), channel_id=1, source_target_pairs={{0,1},{1,2},{2,3},{3,4},{4,5},{5,6},{6,7},{7,0},{8,9},{9,10},{10,1... | collective-permute-start | bytes 737288 | tf_op jit(solution)/shard_map/ppermute | solution.py:50
  78.8 9.4 %collective-permute-start.13 = (bf16[160,768]{1,0:T(8,128)(2,1)S(1)}, bf16[160,768]{1,0:T(8,128)(2,1)S(1)}, u32[]{:S(2)}, u32[]{:S(2)}) collective-permute-start(bf16[160,768]{1,0:T(8,128)(2,1)S(1)} %slice.7), channel_id=1, source_target_pairs={{0,7},{1,0},{2,1},{3,2},{4,3},{5,4},{6,5},{7,6},{8,15},{9,8},{10,9... | collective-permute-start | bytes 737288 | tf_op jit(solution)/shard_map/ppermute | solution.py:50
  89.0 4.3 %collective-permute-start.14 = (f32[384,1280]{1,0:T(8,128)S(1)}, f32[384,1280]{1,0:T(8,128)S(1)}, u32[]{:S(2)}, u32[]{:S(2)}) collective-permute-start(f32[384,1280]{1,0:T(8,128)S(1)} %get-tuple-element.55), channel_id=1, source_target_pairs={{0,8},{8,0},{1,9},{9,1},{2,10},{10,2},{3,11},{11,3},{4,12},{12,4},... | collective-permute-start | bytes 5898248 | tf_op jit(solution)/shard_map/ppermute | solution.py:577
  89.3 4.0 %copy-start = (bf16[384,1,384]{2,0,1:T(8,128)(2,1)S(1)}, bf16[384,1,384]{2,0,1:T(8,128)(2,1)}, u32[]{:S(2)}) copy-start(bf16[384,1,384]{2,0,1:T(8,128)(2,1)} %param.17) | copy-start | bytes 884740
  97.9 2.0 %collective-permute-start.15 = (bf16[384,640]{1,0:T(8,128)(2,1)S(1)}, bf16[384,640]{1,0:T(8,128)(2,1)S(1)}, u32[]{:S(2)}, u32[]{:S(2)}) collective-permute-start(bf16[384,640]{1,0:T(8,128)(2,1)S(1)} %attention.1.own), channel_id=1, source_target_pairs={{0,8},{8,0},{1,9},{9,1},{2,10},{10,2},{3,11},{11,3},{4,12},{12,4},... | collective-permute-start | bytes 1474568 | tf_op jit(solution)/shard_map/ppermute | solution.py:581
  100.5 14.0 %collective-permute-start.18 = (bf16[640,640]{1,0:T(8,128)(2,1)S(1)}, bf16[640,640]{1,0:T(8,128)(2,1)S(1)}, u32[]{:S(2)}, u32[]{:S(2)}) collective-permute-start(bf16[640,640]{1,0:T(8,128)(2,1)S(1)} %rest.1), channel_id=1, source_target_pairs={{0,32},{8,136},{16,48},{24,152},{32,0},{40,168},{48,16},{56,184},{... | collective-permute-start | bytes 2457608 | tf_op jit(solution)/shard_map/ppermute | solution.py:60
  102.2 21.0 %collective-permute-start.17 = (bf16[640,640]{1,0:T(8,128)(2,1)S(1)}, bf16[640,640]{1,0:T(8,128)(2,1)S(1)}, u32[]{:S(2)}, u32[]{:S(2)}) collective-permute-start(bf16[640,640]{1,0:T(8,128)(2,1)S(1)} %gradient.5), channel_id=1, source_target_pairs={{0,16},{8,72},{16,32},{24,88},{32,48},{40,104},{48,0},{56,120},{64... | collective-permute-start | bytes 2457608 | tf_op jit(solution)/shard_map/ppermute | solution.py:60
  106.9 16.3 %collective-permute-start.16 = (bf16[640,640]{1,0:T(8,128)(2,1)S(1)}, bf16[640,640]{1,0:T(8,128)(2,1)S(1)}, u32[]{:S(2)}, u32[]{:S(2)}) collective-permute-start(bf16[640,640]{1,0:T(8,128)(2,1)S(1)} %gradient.4), channel_id=1, source_target_pairs={{0,48},{8,200},{16,0},{24,216},{32,16},{40,232},{48,32},{56,248},{... | collective-permute-start | bytes 2457608 | tf_op jit(solution)/shard_map/ppermute | solution.py:60
  124.1 5.8 %collective-permute-start.19 = (bf16[160,640]{1,0:T(8,128)(2,1)S(1)}, bf16[160,640]{1,0:T(8,128)(2,1)S(1)}, u32[]{:S(2)}, u32[]{:S(2)}) collective-permute-start(bf16[160,640]{1,0:T(8,128)(2,1)S(1)} %get-tuple-element.60), channel_id=1, source_target_pairs={{0,64},{8,24},{16,80},{24,40},{32,96},{40,56},{48,112},{56,8},{64,... | collective-permute-start | bytes 614408 | tf_op jit(solution)/shard_map/ppermute | solution.py:60
  125.2 5.8 %collective-permute-start.20 = (bf16[160,640]{1,0:T(8,128)(2,1)S(1)}, bf16[160,640]{1,0:T(8,128)(2,1)S(1)}, u32[]{:S(2)}, u32[]{:S(2)}) collective-permute-start(bf16[160,640]{1,0:T(8,128)(2,1)S(1)} %get-tuple-element.61), channel_id=1, source_target_pairs={{0,192},{8,56},{16,208},{24,8},{32,224},{40,24},{48,240},{56,40},{... | collective-permute-start | bytes 614408 | tf_op jit(solution)/shard_map/ppermute | solution.py:60
  126.2 7.3 %collective-permute-start.21 = (bf16[160,640]{1,0:T(8,128)(2,1)S(1)}, bf16[160,640]{1,0:T(8,128)(2,1)S(1)}, u32[]{:S(2)}, u32[]{:S(2)}) collective-permute-start(bf16[160,640]{1,0:T(8,128)(2,1)S(1)} %get-tuple-element.62), channel_id=1, source_target_pairs={{0,128},{8,40},{16,144},{24,56},{32,160},{40,8},{48,176},{56,24},{... | collective-permute-start | bytes 614408 | tf_op jit(solution)/shard_map/ppermute | solution.py:60

commit v2 on v1

--- a/solution.py
+++ b/solution.py
@@ -492,29 +492,39 @@
     )(early, rows, other)
 
 
-def middle_kernel(where, own, *refs):
-    pieces, outs = refs[:3], refs[3:]
+def three_sum(own, first, second):
+    def kernel(own, first, second, out):
+        out[...] = own[...].astype(F32) + first[...].astype(F32) + second[...].astype(F32)
+
+    return pl.pallas_call(
+        kernel,
+        out_shape=jax.ShapeDtypeStruct((4 * CHUNK, COLS), F32),
+        in_specs=[VMEM] * 3,
+        out_specs=VMEM,
+        compiler_params=PARAMS,
+        name="three",
+    )(own, first, second)
+
+
+def middle_kernel(where, three, piece, *outs):
     second = turned_place(where)[1]
     for move, out in zip((0, 1, -1, 2), outs):
         at = pl.ds(pl.multiple_of(wrapped(second + move, 4) * CHUNK, 16), CHUNK)
-        total = (own[at, :].astype(F32) + pieces[0][at, :].astype(F32)) + (
-            pieces[1][at, :].astype(F32) + pieces[2][at, :].astype(F32)
-        )
-        out[...] = total.astype(out.dtype)
-
-
-def middle_sums(where, own, pieces):
+        out[...] = (three[at, :] + piece[at, :].astype(F32)).astype(out.dtype)
+
+
+def middle_sums(where, three, piece):
     def shape(kind):
         return jax.ShapeDtypeStruct((CHUNK, COLS), kind)
 
     return pl.pallas_call(
         middle_kernel,
         out_shape=(shape(F32), shape(BF16), shape(BF16), shape(BF16)),
-        in_specs=[SMEM] + [VMEM] * 4,
+        in_specs=[SMEM] + [VMEM] * 2,
         out_specs=(VMEM,) * 4,
         compiler_params=PARAMS,
         name="middle",
-    )(where, own, *pieces)
+    )(where, three, piece)
 
 
 def final_kernel(own, first, second, third, out):
@@ -588,7 +598,7 @@
         else:
             part = gradient_part(small, whole, far, last, grad, grad_other, move)
         parts.append(turned(part, True, move) if move else part)
-    sums = middle_sums(small, parts[3], parts[:3])
+    sums = middle_sums(small, three_sum(parts[3], parts[2], parts[1]), parts[0])
     parts = [turned(part, False, move) for move, part in zip((1, -1, 2), sums[1:])]
     return final_sums(sums[0], parts)
 

time: 135 us -> 137 us (1.015)
  waiting for transfers between devices: 59.7 us -> 61.6 us
    ppermute x12, waiting for transfers between devices: 22.5 us -> 24.5 us  [turned(): return lax.ppermute(value, ('y', 'x', 'c'), pairs)]
  transfers between devices with their start and end apart: 23 -> 23, of which waited for: 13 -> 14; matrix products, arithmetic and copies ran while one was open for 0% -> 0% of each run, Pallas kernels for 15% -> 15%
where the time goes in v2:
time: 137 us; the launch traced here: 136 us
  waiting for transfers between devices  61.6 us (45%)
  starting transfers between devices  41.6 us (30%)
  Pallas kernels  32.8 us (24%)
    ppermute x8, waiting for transfers between devices, shift(): lax.ppermute(value, axis, [(i, (i + by) % size) for i in range(size)])  25.5 us
    ppermute x12, waiting for transfers between devices, turned(): return lax.ppermute(value, ('y', 'x', 'c'), pairs)  24.5 us
    ppermute x8, starting transfers between devices, shift(): lax.ppermute(value, axis, [(i, (i + by) % size) for i in range(size)])  16.7 us
    ppermute x12, starting transfers between devices, turned(): return lax.ppermute(value, ('y', 'x', 'c'), pairs)  16.7 us
    all_to_all x1, waiting for transfers between devices, body(): lax.all_to_all(outgoing, ('y', 'x', 'c'), split_axis=0, concat_axis=0, ti...  11.1 us
    all_to_all x1, starting transfers between devices, body(): lax.all_to_all(outgoing, ('y', 'x', 'c'), split_axis=0, concat_axis=0, ti...  7.68 us
    pallas_call x3, Pallas kernels, gradient_part(): pl.pallas_call(kernel, out_shape=PART, in_specs=[SMEM] + [VMEM] * 5, out_...  4.83 us
    pallas_call x1, Pallas kernels, attention(): pl.pallas_call(attention_kernel, out_shape=jax.ShapeDtypeStruct((ROWS, CO...  4.63 us
  transfers between devices with their start and end apart: 23, of which 14 were waited for; matrix products, arithmetic and copies ran while one was open for 0% of the time, Pallas kernels for 15%

profile of v2, /device:TPU:8, one launch (start us, length us, event | category | flops | bytes accessed | tf_op | source)
XLA Modules:
  0.0 136.5 jit_solution(16799636684065858146)
XLA Ops:
  0.0 4.2 %route.1 = bf16[32,48,384]{2,1,0:T(8,128)(2,1)} custom-call(s32[4]{0:T(128)} %rewards.1, s32[4]{0:T(128)} %groups.1, s32[384]{0:T(512)} %shard.1, s32[384]{0:T(512)} %offset.1, bf16[384,640]{1,0:T(8,128)(2,1)} %tokens.1), custom_call_target="tpu_custom_call" | custom-call | tf_op jit(solution)/shard_map/route/pallas_call | solution.py:115
  4.2 7.7 %all-to-all-start = ((bf16[32,48,384]{2,1,0:T(8,128)(2,1)}), bf16[32,48,384]{2,1,0:T(8,128)(2,1)S(1)}, u32[]{:S(2)}, u32[]{:S(2)}) async-start(bf16[32,48,384]{2,1,0:T(8,128)(2,1)} %route.1), calls=%async_computation | async-start | bytes 2359296 | tf_op jit(solution)/shard_map/all_to_all | solution.py:559
  12.0 1.5 %collective-permute-start.4 = (bf16[160,1280]{1,0:T(8,128)(2,1)S(1)}, bf16[160,1280]{1,0:T(8,128)(2,1)S(1)}, u32[]{:S(2)}, u32[]{:S(2)}) collective-permute-start(bf16[160,1280]{1,0:T(8,128)(2,1)S(1)} %constant_dynamic-update-slice_fusion.refs_0_), channel_id=1, source_target_pairs={{0,16},{8,72},{16,32},{24,88},{32,48},{40,104},{48,0},{56,120},{64... | collective-permute-start | bytes 1228808 | tf_op jit(solution)/shard_map/ppermute | solution.py:60
  13.5 1.8 %collective-permute-start.5 = (bf16[160,1280]{1,0:T(8,128)(2,1)S(1)}, bf16[160,1280]{1,0:T(8,128)(2,1)S(1)}, u32[]{:S(2)}, u32[]{:S(2)}) collective-permute-start(bf16[160,1280]{1,0:T(8,128)(2,1)S(1)} %constant_dynamic-update-slice_fusion.refs_0_), channel_id=1, source_target_pairs={{0,48},{8,200},{16,0},{24,216},{32,16},{40,232},{48,32},{56,248},{... | collective-permute-start | bytes 1228808 | tf_op jit(solution)/shard_map/ppermute | solution.py:60
  15.3 1.8 %collective-permute-start.6 = (bf16[160,1280]{1,0:T(8,128)(2,1)S(1)}, bf16[160,1280]{1,0:T(8,128)(2,1)S(1)}, u32[]{:S(2)}, u32[]{:S(2)}) collective-permute-start(bf16[160,1280]{1,0:T(8,128)(2,1)S(1)} %constant_dynamic-update-slice_fusion.refs_0_), channel_id=1, source_target_pairs={{0,32},{8,136},{16,48},{24,152},{32,0},{40,168},{48,16},{56,184},{... | collective-permute-start | bytes 1228808 | tf_op jit(solution)/shard_map/ppermute | solution.py:60
  17.2 11.1 %all-to-all-done.arrived = bf16[32,48,384]{2,1,0:T(8,128)(2,1)S(1)} async-done(((bf16[32,48,384]{2,1,0:T(8,128)(2,1)}), bf16[32,48,384]{2,1,0:T(8,128)(2,1)S(1)}, u32[]{:S(2)}, u32[]{:S(2)}) %all-to-all-start) | async-done | bytes 1179680 | tf_op jit(solution)/shard_map/all_to_all | solution.py:559
  28.2 1.6 %place.1.refs_2_ = bf16[320,768]{1,0:T(8,128)(2,1)S(1)} custom-call(bf16[32,48,384]{2,1,0:T(8,128)(2,1)S(1)} %all-to-all-done.arrived), custom_call_target="tpu_custom_call" | custom-call | tf_op jit(solution)/shard_map/place/pallas_call | solution.py:137
  29.8 5.9 %collective-permute-start.2 = (bf16[320,768]{1,0:T(8,128)(2,1)S(1)}, bf16[320,768]{1,0:T(8,128)(2,1)S(1)}, u32[]{:S(2)}, u32[]{:S(2)}) collective-permute-start(bf16[320,768]{1,0:T(8,128)(2,1)S(1)} %place.1.refs_2_), channel_id=1, source_target_pairs={{0,7},{1,0},{2,1},{3,2},{4,3},{5,4},{6,5},{7,6},{8,15},{9,8},{10,9... | collective-permute-start | bytes 1474568 | tf_op jit(solution)/shard_map/ppermute | solution.py:50
  35.8 2.0 %collective-permute-done.6.refs_3_ = bf16[160,1280]{1,0:T(8,128)(2,1)S(1)} collective-permute-done((bf16[160,1280]{1,0:T(8,128)(2,1)S(1)}, bf16[160,1280]{1,0:T(8,128)(2,1)S(1)}, u32[]{:S(2)}, u32[]{:S(2)}) %collective-permute-start.6) | collective-permute-done | bytes 409632 | tf_op jit(solution)/shard_map/ppermute | solution.py:60
  39.0 1.6 %collective-permute-start.11 = (bf16[640,1280]{1,0:T(8,128)(2,1)S(1)}, bf16[640,1280]{1,0:T(8,128)(2,1)S(1)}, u32[]{:S(2)}, u32[]{:S(2)}) collective-permute-start(bf16[640,1280]{1,0:T(8,128)(2,1)S(1)} %join.1.refs_5_.refs_2_), channel_id=1, source_target_pairs={{0,128},{8,40},{16,144},{24,56},{32,160},{40,8},{48,176},{56,24},{... | collective-permute-start | bytes 4915208 | tf_op jit(solution)/shard_map/ppermute | solution.py:60
  40.6 2.0 %collective-permute-start.9 = (bf16[640,1280]{1,0:T(8,128)(2,1)S(1)}, bf16[640,1280]{1,0:T(8,128)(2,1)S(1)}, u32[]{:S(2)}, u32[]{:S(2)}) collective-permute-start(bf16[640,1280]{1,0:T(8,128)(2,1)S(1)} %join.1.refs_5_.refs_2_), channel_id=1, source_target_pairs={{0,64},{8,24},{16,80},{24,40},{32,96},{40,56},{48,112},{56,8},{64,... | collective-permute-start | bytes 4915208 | tf_op jit(solution)/shard_map/ppermute | solution.py:60
  42.7 4.7 %collective-permute-done.2.refs_3_ = bf16[320,768]{1,0:T(8,128)(2,1)S(1)} collective-permute-done((bf16[320,768]{1,0:T(8,128)(2,1)S(1)}, bf16[320,768]{1,0:T(8,128)(2,1)S(1)}, u32[]{:S(2)}, u32[]{:S(2)}) %collective-permute-start.2) | collective-permute-done | bytes 491552 | tf_op jit(solution)/shard_map/ppermute | solution.py:50
  47.3 3.7 %collective-permute-start.3 = (bf16[320,768]{1,0:T(8,128)(2,1)S(1)}, bf16[320,768]{1,0:T(8,128)(2,1)S(1)}, u32[]{:S(2)}, u32[]{:S(2)}) collective-permute-start(bf16[320,768]{1,0:T(8,128)(2,1)S(1)} %collective-permute-done.2.refs_3_), channel_id=1, source_target_pairs={{0,7},{1,0},{2,1},{3,2},{4,3},{5,4},{6,5},{7,6},{8,15},{9,8},{10,9... | collective-permute-start | bytes 1474568 | tf_op jit(solution)/shard_map/ppermute | solution.py:50
  51.0 10.7 %collective-permute-done.3.refs_4_ = bf16[320,768]{1,0:T(8,128)(2,1)S(1)} collective-permute-done((bf16[320,768]{1,0:T(8,128)(2,1)S(1)}, bf16[320,768]{1,0:T(8,128)(2,1)S(1)}, u32[]{:S(2)}, u32[]{:S(2)}) %collective-permute-start.3) | collective-permute-done | bytes 491552 | tf_op jit(solution)/shard_map/ppermute | solution.py:50
  61.7 3.7 %collective-permute-start.7 = (bf16[320,768]{1,0:T(8,128)(2,1)S(1)}, bf16[320,768]{1,0:T(8,128)(2,1)S(1)}, u32[]{:S(2)}, u32[]{:S(2)}) collective-permute-start(bf16[320,768]{1,0:T(8,128)(2,1)S(1)} %collective-permute-done.3.refs_4_), channel_id=1, source_target_pairs={{0,7},{1,0},{2,1},{3,2},{4,3},{5,4},{6,5},{7,6},{8,15},{9,8},{10,9... | collective-permute-start | bytes 1474568 | tf_op jit(solution)/shard_map/ppermute | solution.py:50
  65.4 3.1 %project.1 = (f32[384,1280]{1,0:T(8,128)S(1)}, f32[384,1280]{1,0:T(8,128)S(1)}, bf16[320,1280]{1,0:T(8,128)(2,1)S(1)}, f32[384,128]{1,0:T(8,128)S(1)}, bf16[1600,768]{1,0:T(8,128)(2,1)S(1)}) custom-call(s32[16]{0:T(128)S(1)} %concatenate.6.where.small, bf16[32,48,384]{2,1,0:T(8,128)(2,1)S(1)} %all-to-all-done.arrived, ...), custom_call_target="tpu_custom_call" | custom-call | tf_op jit(solution)/shard_map/project/pallas_call | solution.py:254
  68.5 6.8 %collective-permute-done.7.refs_0_ = bf16[320,768]{1,0:T(8,128)(2,1)S(1)} collective-permute-done((bf16[320,768]{1,0:T(8,128)(2,1)S(1)}, bf16[320,768]{1,0:T(8,128)(2,1)S(1)}, u32[]{:S(2)}, u32[]{:S(2)}) %collective-permute-start.7) | collective-permute-done | bytes 491552 | tf_op jit(solution)/shard_map/ppermute | solution.py:50
  75.3 3.4 %collective-permute-done.8.refs_1_ = bf16[320,768]{1,0:T(8,128)(2,1)S(1)} collective-permute-done((bf16[320,768]{1,0:T(8,128)(2,1)S(1)}, bf16[320,768]{1,0:T(8,128)(2,1)S(1)}, u32[]{:S(2)}, u32[]{:S(2)}) %collective-permute-start.8) | collective-permute-done | bytes 491552 | tf_op jit(solution)/shard_map/ppermute | solution.py:50
  78.8 3.3 %collective-permute-start.13 = (bf16[160,768]{1,0:T(8,128)(2,1)S(1)}, bf16[160,768]{1,0:T(8,128)(2,1)S(1)}, u32[]{:S(2)}, u32[]{:S(2)}) collective-permute-start(bf16[160,768]{1,0:T(8,128)(2,1)S(1)} %slice.7), channel_id=1, source_target_pairs={{0,7},{1,0},{2,1},{3,2},{4,3},{5,4},{6,5},{7,6},{8,15},{9,8},{10,9... | collective-permute-start | bytes 737288 | tf_op jit(solution)/shard_map/ppermute | solution.py:50
  82.1 2.4 %far.1 = (f32[384,1280]{1,0:T(8,128)S(1)}, f32[384,1280]{1,0:T(8,128)S(1)}, bf16[640,768]{1,0:T(8,128)(2,1)S(1)}) custom-call(s32[16]{0:T(128)S(1)} %concatenate.6.where.small, f32[384,1280]{1,0:T(8,128)S(1)} %get-tuple-element.44.own, f32[384,1280]{1,0:T(8,128)S(1)} %get-tuple-element.45.other, bf16[320,768]{1,0:T(8,128)(2,1)S(1)} %collective-permute-done.7.refs_0_, ...), custom_call_target="tpu_custom_call" | custom-call | tf_op jit(solution)/shard_map/far/pallas_call | solution.py:288
  84.5 3.7 %across_other.1 = (f32[384,1280]{1,0:T(8,128)S(1)}, bf16[320,1280]{1,0:T(8,128)(2,1)S(1)}) custom-call(s32[16]{0:T(128)S(1)} %concatenate.6.where.small, f32[384,1280]{1,0:T(8,128)S(1)} %get-tuple-element.47.other, bf16[320,1280]{1,0:T(8,128)(2,1)S(1)} %get-tuple-element.48.late, bf16[1600,768]{1,0:T(8,128)(2,1)S(1)} %get-tuple-element.42.whole, ...), custom_call_target="tpu_custom_call" | custom-call | tf_op jit(solution)/shard_map/across_other/pallas_call | solution.py:316
  89.3 3.7 %across_own.1.own = f32[384,1280]{1,0:T(8,128)S(1)} custom-call(s32[16]{0:T(128)S(1)} %concatenate.6.where.small, f32[384,1280]{1,0:T(8,128)S(1)} %get-tuple-element.54.own, bf16[320,1280]{1,0:T(8,128)(2,1)S(1)} %get-tuple-element.50.late, bf16[1600,768]{1,0:T(8,128)(2,1)S(1)} %get-tuple-element.42.whole, bf16[640,768]{1,0:T(8,128)(2,1)S(1)} %get-tuple-element.46.far, ...), custom_call_target="tpu_custom_call" | custom-call | tf_op jit(solution)/shard_map/across_own/pallas_call | solution.py:347
  93.3 4.6 %attention.1.own = bf16[384,640]{1,0:T(8,128)(2,1)S(1)} custom-call(s32[16]{0:T(128)S(1)} %concatenate.6.where.small, f32[384,1280]{1,0:T(8,128)S(1)} %across_own.1.own, f32[384,1280]{1,0:T(8,128)S(1)} %collective-permute-done.14.received, bf16[384,384]{1,0:T(8,128)(2,1)S(1)} %bitcast.8, f32[384,128]{1,0:T(8,128)S(1)} %get-tuple-element.56.advantage), custom_call_target="tpu_custom_call" | custom-call | tf_op jit(solution)/shard_map/attention/pallas_call | solution.py:418
  98.2 1.4 early.1
  99.8 1.6 %gradient.4 = bf16[640,640]{1,0:T(8,128)(2,1)S(1)} custom-call(s32[16]{0:T(128)S(1)} %concatenate.6.where.small, bf16[1600,768]{1,0:T(8,128)(2,1)S(1)} %get-tuple-element.42.whole, bf16[640,768]{1,0:T(8,128)(2,1)S(1)} %get-tuple-element.46.far, bf16[320,768]{1,0:T(8,128)(2,1)S(1)} %get-tuple-element.53.last, bf16[384,640]{1,0:T(8,128)(2,1)S(1)} %attention.1.own, ...), custom_call_target="tpu_custom_call" | custom-call | tf_op jit(solution)/shard_map/gradient/pallas_call | solution.py:446
  103.1 2.8 %collective-permute-start.16 = (bf16[640,640]{1,0:T(8,128)(2,1)S(1)}, bf16[640,640]{1,0:T(8,128)(2,1)S(1)}, u32[]{:S(2)}, u32[]{:S(2)}) collective-permute-start(bf16[640,640]{1,0:T(8,128)(2,1)S(1)} %rest.1), channel_id=1, source_target_pairs={{0,32},{8,136},{16,48},{24,152},{32,0},{40,168},{48,16},{56,184},{... | collective-permute-start | bytes 2457608 | tf_op jit(solution)/shard_map/ppermute | solution.py:60
  105.9 1.6 %gradient.5 = bf16[640,640]{1,0:T(8,128)(2,1)S(1)} custom-call(s32[16]{0:T(128)S(1)} %concatenate.6.where.small, bf16[1600,768]{1,0:T(8,128)(2,1)S(1)} %get-tuple-element.42.whole, bf16[640,768]{1,0:T(8,128)(2,1)S(1)} %get-tuple-element.46.far, bf16[320,768]{1,0:T(8,128)(2,1)S(1)} %get-tuple-element.53.last, bf16[384,640]{1,0:T(8,128)(2,1)S(1)} %attention.1.own, ...), custom_call_target="tpu_custom_call" | custom-call | tf_op jit(solution)/shard_map/gradient/pallas_call | solution.py:446
  107.8 1.6 %gradient.3.own = bf16[640,640]{1,0:T(8,128)(2,1)S(1)} custom-call(s32[16]{0:T(128)S(1)} %concatenate.6.where.small, bf16[1600,768]{1,0:T(8,128)(2,1)S(1)} %get-tuple-element.42.whole, bf16[640,768]{1,0:T(8,128)(2,1)S(1)} %get-tuple-element.46.far, bf16[320,768]{1,0:T(8,128)(2,1)S(1)} %get-tuple-element.53.last, bf16[384,640]{1,0:T(8,128)(2,1)S(1)} %attention.1.own, ...), custom_call_target="tpu_custom_call" | custom-call | tf_op jit(solution)/shard_map/gradient/pallas_call | solution.py:446
  109.5 5.6 %collective-permute-done.17.second = bf16[640,640]{1,0:T(8,128)(2,1)S(1)} collective-permute-done((bf16[640,640]{1,0:T(8,128)(2,1)S(1)}, bf16[640,640]{1,0:T(8,128)(2,1)S(1)}, u32[]{:S(2)}, u32[]{:S(2)}) %collective-permute-start.17) | collective-permute-done | bytes 819232 | tf_op jit(solution)/shard_map/ppermute | solution.py:60
  115.1 9.2 %collective-permute-done.16.first = bf16[640,640]{1,0:T(8,128)(2,1)S(1)} collective-permute-done((bf16[640,640]{1,0:T(8,128)(2,1)S(1)}, bf16[640,640]{1,0:T(8,128)(2,1)S(1)}, u32[]{:S(2)}, u32[]{:S(2)}) %collective-permute-start.16) | collective-permute-done | bytes 819232 | tf_op jit(solution)/shard_map/ppermute | solution.py:60
  128.8 3.2 %collective-permute-done.19.first = bf16[160,640]{1,0:T(8,128)(2,1)S(1)} collective-permute-done((bf16[160,640]{1,0:T(8,128)(2,1)S(1)}, bf16[160,640]{1,0:T(8,128)(2,1)S(1)}, u32[]{:S(2)}, u32[]{:S(2)}) %collective-permute-start.19) | collective-permute-done | bytes 204832 | tf_op jit(solution)/shard_map/ppermute | solution.py:60
  133.0 2.5 %collective-permute-done.21.third = bf16[160,640]{1,0:T(8,128)(2,1)S(1)} collective-permute-done((bf16[160,640]{1,0:T(8,128)(2,1)S(1)}, bf16[160,640]{1,0:T(8,128)(2,1)S(1)}, u32[]{:S(2)}, u32[]{:S(2)}) %collective-permute-start.21) | collective-permute-done | bytes 204832 | tf_op jit(solution)/shard_map/ppermute | solution.py:60
  (48 shorter events, 11.9 us)
Async XLA Ops:
  0.0 11.9 %copy-start.1 = (bf16[160,1,640]{2,0,1:T(8,128)(2,1)S(1)}, bf16[160,1,640]{2,0,1:T(8,128)(2,1)}, u32[]{:S(2)}) copy-start(bf16[160,1,640]{2,0,1:T(8,128)(2,1)} %param.15) | copy-start | bytes 614404
  0.0 12.0 %copy-start.2 = (bf16[160,1,640]{2,0,1:T(8,128)(2,1)S(1)}, bf16[160,1,640]{2,0,1:T(8,128)(2,1)}, u32[]{:S(2)}) copy-start(bf16[160,1,640]{2,0,1:T(8,128)(2,1)} %param.16) | copy-start | bytes 614404
  4.2 12.9 %copy-start.3 = (s32[4]{0:T(128)S(1)}, s32[4]{0:T(128)}, u32[]{:S(2)}) copy-start(s32[4]{0:T(128)} %rewards.1) | copy-start | bytes 52
  4.2 12.9 %copy-start.4 = (s32[4]{0:T(128)S(1)}, s32[4]{0:T(128)}, u32[]{:S(2)}) copy-start(s32[4]{0:T(128)} %groups.1) | copy-start | bytes 52
  4.2 12.9 %copy-start.5 = (s32[1,4]{1,0:T(1,128)S(1)}, s32[1,4]{1,0:T(1,128)}, u32[]{:S(2)}) copy-start(s32[1,4]{1,0:T(1,128)} %param.12) | copy-start | bytes 52
  4.2 24.0 %all-to-all-start = ((bf16[32,48,384]{2,1,0:T(8,128)(2,1)}), bf16[32,48,384]{2,1,0:T(8,128)(2,1)S(1)}, u32[]{:S(2)}, u32[]{:S(2)}) async-start(bf16[32,48,384]{2,1,0:T(8,128)(2,1)} %route.1), calls=%async_computation | async-start | bytes 2359296 | tf_op jit(solution)/shard_map/all_to_all | solution.py:559
  12.0 23.8 %collective-permute-start.4 = (bf16[160,1280]{1,0:T(8,128)(2,1)S(1)}, bf16[160,1280]{1,0:T(8,128)(2,1)S(1)}, u32[]{:S(2)}, u32[]{:S(2)}) collective-permute-start(bf16[160,1280]{1,0:T(8,128)(2,1)S(1)} %constant_dynamic-update-slice_fusion.refs_0_), channel_id=1, source_target_pairs={{0,16},{8,72},{16,32},{24,88},{32,48},{40,104},{48,0},{56,120},{64... | collective-permute-start | bytes 1228808 | tf_op jit(solution)/shard_map/ppermute | solution.py:60
  13.5 22.2 %collective-permute-start.5 = (bf16[160,1280]{1,0:T(8,128)(2,1)S(1)}, bf16[160,1280]{1,0:T(8,128)(2,1)S(1)}, u32[]{:S(2)}, u32[]{:S(2)}) collective-permute-start(bf16[160,1280]{1,0:T(8,128)(2,1)S(1)} %constant_dynamic-update-slice_fusion.refs_0_), channel_id=1, source_target_pairs={{0,48},{8,200},{16,0},{24,216},{32,16},{40,232},{48,32},{56,248},{... | collective-permute-start | bytes 1228808 | tf_op jit(solution)/shard_map/ppermute | solution.py:60
  15.3 22.5 %collective-permute-start.6 = (bf16[160,1280]{1,0:T(8,128)(2,1)S(1)}, bf16[160,1280]{1,0:T(8,128)(2,1)S(1)}, u32[]{:S(2)}, u32[]{:S(2)}) collective-permute-start(bf16[160,1280]{1,0:T(8,128)(2,1)S(1)} %constant_dynamic-update-slice_fusion.refs_0_), channel_id=1, source_target_pairs={{0,32},{8,136},{16,48},{24,152},{32,0},{40,168},{48,16},{56,184},{... | collective-permute-start | bytes 1228808 | tf_op jit(solution)/shard_map/ppermute | solution.py:60
  29.8 17.5 %collective-permute-start.2 = (bf16[320,768]{1,0:T(8,128)(2,1)S(1)}, bf16[320,768]{1,0:T(8,128)(2,1)S(1)}, u32[]{:S(2)}, u32[]{:S(2)}) collective-permute-start(bf16[320,768]{1,0:T(8,128)(2,1)S(1)} %place.1.refs_2_), channel_id=1, source_target_pairs={{0,7},{1,0},{2,1},{3,2},{4,3},{5,4},{6,5},{7,6},{8,15},{9,8},{10,9... | collective-permute-start | bytes 1474568 | tf_op jit(solution)/shard_map/ppermute | solution.py:50
  35.8 15.3 %collective-permute-start = (bf16[320,768]{1,0:T(8,128)(2,1)S(1)}, bf16[320,768]{1,0:T(8,128)(2,1)S(1)}, u32[]{:S(2)}, u32[]{:S(2)}) collective-permute-start(bf16[320,768]{1,0:T(8,128)(2,1)S(1)} %place.1.refs_2_), channel_id=1, source_target_pairs={{0,1},{1,2},{2,3},{3,4},{4,5},{5,6},{6,7},{7,0},{8,9},{9,10},{10,1... | collective-permute-start | bytes 1474568 | tf_op jit(solution)/shard_map/ppermute | solution.py:50
  37.9 46.6 %collective-permute-start.10 = (bf16[640,1280]{1,0:T(8,128)(2,1)S(1)}, bf16[640,1280]{1,0:T(8,128)(2,1)S(1)}, u32[]{:S(2)}, u32[]{:S(2)}) collective-permute-start(bf16[640,1280]{1,0:T(8,128)(2,1)S(1)} %join.1.refs_5_.refs_2_), channel_id=1, source_target_pairs={{0,192},{8,56},{16,208},{24,8},{32,224},{40,24},{48,240},{56,40},{... | collective-permute-start | bytes 4915208 | tf_op jit(solution)/shard_map/ppermute | solution.py:60
  39.0 45.5 %collective-permute-start.11 = (bf16[640,1280]{1,0:T(8,128)(2,1)S(1)}, bf16[640,1280]{1,0:T(8,128)(2,1)S(1)}, u32[]{:S(2)}, u32[]{:S(2)}) collective-permute-start(bf16[640,1280]{1,0:T(8,128)(2,1)S(1)} %join.1.refs_5_.refs_2_), channel_id=1, source_target_pairs={{0,128},{8,40},{16,144},{24,56},{32,160},{40,8},{48,176},{56,24},{... | collective-permute-start | bytes 4915208 | tf_op jit(solution)/shard_map/ppermute | solution.py:60
  40.6 43.9 %collective-permute-start.9 = (bf16[640,1280]{1,0:T(8,128)(2,1)S(1)}, bf16[640,1280]{1,0:T(8,128)(2,1)S(1)}, u32[]{:S(2)}, u32[]{:S(2)}) collective-permute-start(bf16[640,1280]{1,0:T(8,128)(2,1)S(1)} %join.1.refs_5_.refs_2_), channel_id=1, source_target_pairs={{0,64},{8,24},{16,80},{24,40},{32,96},{40,56},{48,112},{56,8},{64,... | collective-permute-start | bytes 4915208 | tf_op jit(solution)/shard_map/ppermute | solution.py:60
  47.3 14.4 %collective-permute-start.3 = (bf16[320,768]{1,0:T(8,128)(2,1)S(1)}, bf16[320,768]{1,0:T(8,128)(2,1)S(1)}, u32[]{:S(2)}, u32[]{:S(2)}) collective-permute-start(bf16[320,768]{1,0:T(8,128)(2,1)S(1)} %collective-permute-done.2.refs_3_), channel_id=1, source_target_pairs={{0,7},{1,0},{2,1},{3,2},{4,3},{5,4},{6,5},{7,6},{8,15},{9,8},{10,9... | collective-permute-start | bytes 1474568 | tf_op jit(solution)/shard_map/ppermute | solution.py:50
  51.0 14.4 %collective-permute-start.1 = (bf16[320,768]{1,0:T(8,128)(2,1)S(1)}, bf16[320,768]{1,0:T(8,128)(2,1)S(1)}, u32[]{:S(2)}, u32[]{:S(2)}) collective-permute-start(bf16[320,768]{1,0:T(8,128)(2,1)S(1)} %collective-permute-done.refs_1_), channel_id=1, source_target_pairs={{0,1},{1,2},{2,3},{3,4},{4,5},{5,6},{6,7},{7,0},{8,9},{9,10},{10,1... | collective-permute-start | bytes 1474568 | tf_op jit(solution)/shard_map/ppermute | solution.py:50
  61.7 13.6 %collective-permute-start.7 = (bf16[320,768]{1,0:T(8,128)(2,1)S(1)}, bf16[320,768]{1,0:T(8,128)(2,1)S(1)}, u32[]{:S(2)}, u32[]{:S(2)}) collective-permute-start(bf16[320,768]{1,0:T(8,128)(2,1)S(1)} %collective-permute-done.3.refs_4_), channel_id=1, source_target_pairs={{0,7},{1,0},{2,1},{3,2},{4,3},{5,4},{6,5},{7,6},{8,15},{9,8},{10,9... | collective-permute-start | bytes 1474568 | tf_op jit(solution)/shard_map/ppermute | solution.py:50
  65.4 13.3 %collective-permute-start.8 = (bf16[320,768]{1,0:T(8,128)(2,1)S(1)}, bf16[320,768]{1,0:T(8,128)(2,1)S(1)}, u32[]{:S(2)}, u32[]{:S(2)}) collective-permute-start(bf16[320,768]{1,0:T(8,128)(2,1)S(1)} %collective-permute-done.1.refs_0_), channel_id=1, source_target_pairs={{0,1},{1,2},{2,3},{3,4},{4,5},{5,6},{6,7},{7,0},{8,9},{9,10},{10,1... | collective-permute-start | bytes 1474568 | tf_op jit(solution)/shard_map/ppermute | solution.py:50
  78.7 9.5 %collective-permute-start.12 = (bf16[160,768]{1,0:T(8,128)(2,1)S(1)}, bf16[160,768]{1,0:T(8,128)(2,1)S(1)}, u32[]{:S(2)}, u32[]{:S(2)}) collective-permute-start(bf16[160,768]{1,0:T(8,128)(2,1)S(1)} %slice.6), channel_id=1, source_target_pairs={{0,1},{1,2},{2,3},{3,4},{4,5},{5,6},{6,7},{7,0},{8,9},{9,10},{10,1... | collective-permute-start | bytes 737288 | tf_op jit(solution)/shard_map/ppermute | solution.py:50
  78.8 9.4 %collective-permute-start.13 = (bf16[160,768]{1,0:T(8,128)(2,1)S(1)}, bf16[160,768]{1,0:T(8,128)(2,1)S(1)}, u32[]{:S(2)}, u32[]{:S(2)}) collective-permute-start(bf16[160,768]{1,0:T(8,128)(2,1)S(1)} %slice.7), channel_id=1, source_target_pairs={{0,7},{1,0},{2,1},{3,2},{4,3},{5,4},{6,5},{7,6},{8,15},{9,8},{10,9... | collective-permute-start | bytes 737288 | tf_op jit(solution)/shard_map/ppermute | solution.py:50
  89.0 4.3 %collective-permute-start.14 = (f32[384,1280]{1,0:T(8,128)S(1)}, f32[384,1280]{1,0:T(8,128)S(1)}, u32[]{:S(2)}, u32[]{:S(2)}) collective-permute-start(f32[384,1280]{1,0:T(8,128)S(1)} %get-tuple-element.55), channel_id=1, source_target_pairs={{0,8},{8,0},{1,9},{9,1},{2,10},{10,2},{3,11},{11,3},{4,12},{12,4},... | collective-permute-start | bytes 5898248 | tf_op jit(solution)/shard_map/ppermute | solution.py:587
  89.3 4.0 %copy-start = (bf16[384,1,384]{2,0,1:T(8,128)(2,1)S(1)}, bf16[384,1,384]{2,0,1:T(8,128)(2,1)}, u32[]{:S(2)}) copy-start(bf16[384,1,384]{2,0,1:T(8,128)(2,1)} %param.17) | copy-start | bytes 884740
  97.9 2.0 %collective-permute-start.15 = (bf16[384,640]{1,0:T(8,128)(2,1)S(1)}, bf16[384,640]{1,0:T(8,128)(2,1)S(1)}, u32[]{:S(2)}, u32[]{:S(2)}) collective-permute-start(bf16[384,640]{1,0:T(8,128)(2,1)S(1)} %attention.1.own), channel_id=1, source_target_pairs={{0,8},{8,0},{1,9},{9,1},{2,10},{10,2},{3,11},{11,3},{4,12},{12,4},... | collective-permute-start | bytes 1474568 | tf_op jit(solution)/shard_map/ppermute | solution.py:591
  101.5 13.6 %collective-permute-start.17 = (bf16[640,640]{1,0:T(8,128)(2,1)S(1)}, bf16[640,640]{1,0:T(8,128)(2,1)S(1)}, u32[]{:S(2)}, u32[]{:S(2)}) collective-permute-start(bf16[640,640]{1,0:T(8,128)(2,1)S(1)} %gradient.4), channel_id=1, source_target_pairs={{0,16},{8,72},{16,32},{24,88},{32,48},{40,104},{48,0},{56,120},{64... | collective-permute-start | bytes 2457608 | tf_op jit(solution)/shard_map/ppermute | solution.py:60
  103.1 21.2 %collective-permute-start.16 = (bf16[640,640]{1,0:T(8,128)(2,1)S(1)}, bf16[640,640]{1,0:T(8,128)(2,1)S(1)}, u32[]{:S(2)}, u32[]{:S(2)}) collective-permute-start(bf16[640,640]{1,0:T(8,128)(2,1)S(1)} %rest.1), channel_id=1, source_target_pairs={{0,32},{8,136},{16,48},{24,152},{32,0},{40,168},{48,16},{56,184},{... | collective-permute-start | bytes 2457608 | tf_op jit(solution)/shard_map/ppermute | solution.py:60
  107.5 18.0 %collective-permute-start.18 = (bf16[640,640]{1,0:T(8,128)(2,1)S(1)}, bf16[640,640]{1,0:T(8,128)(2,1)S(1)}, u32[]{:S(2)}, u32[]{:S(2)}) collective-permute-start(bf16[640,640]{1,0:T(8,128)(2,1)S(1)} %gradient.5), channel_id=1, source_target_pairs={{0,48},{8,200},{16,0},{24,216},{32,16},{40,232},{48,32},{56,248},{... | collective-permute-start | bytes 2457608 | tf_op jit(solution)/shard_map/ppermute | solution.py:60
  126.2 5.8 %collective-permute-start.19 = (bf16[160,640]{1,0:T(8,128)(2,1)S(1)}, bf16[160,640]{1,0:T(8,128)(2,1)S(1)}, u32[]{:S(2)}, u32[]{:S(2)}) collective-permute-start(bf16[160,640]{1,0:T(8,128)(2,1)S(1)} %get-tuple-element.60), channel_id=1, source_target_pairs={{0,64},{8,24},{16,80},{24,40},{32,96},{40,56},{48,112},{56,8},{64,... | collective-permute-start | bytes 614408 | tf_op jit(solution)/shard_map/ppermute | solution.py:60
  127.3 5.8 %collective-permute-start.20 = (bf16[160,640]{1,0:T(8,128)(2,1)S(1)}, bf16[160,640]{1,0:T(8,128)(2,1)S(1)}, u32[]{:S(2)}, u32[]{:S(2)}) collective-permute-start(bf16[160,640]{1,0:T(8,128)(2,1)S(1)} %get-tuple-element.61), channel_id=1, source_target_pairs={{0,192},{8,56},{16,208},{24,8},{32,224},{40,24},{48,240},{56,40},{... | collective-permute-start | bytes 614408 | tf_op jit(solution)/shard_map/ppermute | solution.py:60
  128.3 7.3 %collective-permute-start.21 = (bf16[160,640]{1,0:T(8,128)(2,1)S(1)}, bf16[160,640]{1,0:T(8,128)(2,1)S(1)}, u32[]{:S(2)}, u32[]{:S(2)}) collective-permute-start(bf16[160,640]{1,0:T(8,128)(2,1)S(1)} %get-tuple-element.62), channel_id=1, source_target_pairs={{0,128},{8,40},{16,144},{24,56},{32,160},{40,8},{48,176},{56,24},{... | collective-permute-start | bytes 614408 | tf_op jit(solution)/shard_map/ppermute | solution.py:60
